TPU v7x, 32 devices: a whole 2x2x4 slice. The times are simulated.
32 devices in a mesh: expert: 16 (over z, x, core), tensor: 2 (over y).
Axes of the slice: x: 2, y: 2, z: 4, core: 2. Of those that a mesh axis runs over, the one named last changes fastest.
Arguments:
- tokens: bfloat16 [2048, 7168], P('expert', 'tensor'), may hold values from -6 to 6
- route_ids: int32 [2048, 8], P('expert'), may hold values from 0 to 255, as said below
- route_weight: float32 [2048, 8], P('expert'), may hold values from 0.1 to 2.5
- gate_up: bfloat16 [16, 2, 7168, 1024], P('expert', None, None, 'tensor'), may hold values from -0.0625 to 0.0625
- block_keep: int32 [16, 2, 112, 16], P('expert', None, None, 'tensor'), may hold values 0 or 1
Outputs:
- hidden_slots: bfloat16 [16, 128, 1024], P('expert', None, 'tensor')
Inputs may be any that keep to these rules, and one draw needn't show every extreme that they name: `route_ids`: each row names 8 different experts. Within each aligned block of 128 rows no expert is named by more than 8 rows, and one expert numbered below 16 is named by exactly 8 rows in every block.
All inputs are finite; a program needn't handle non-finite values. No bound on the sum of `block_keep` on one device may be relied on, other than what follows from the above.
Results may differ from a plain program's by a relative error of at most 0.0051.
Values may be sent and summed in bfloat16 or wider, within the bound.
No kernel may reach another device: no remote copies, remote signals or barrier semaphores. Data moves between devices by JAX's collectives and lax.ppermute only.
A program may use at most 64 MiB of HBM per device.

v0:
```python
import jax
import jax.numpy as jnp
from jax import lax
from jax.sharding import PartitionSpec as P

BLOCK = 64
CAP = 8


def expand_mask(keep_mask, block_size):
    widened = jnp.repeat(keep_mask, block_size, axis=1)
    return jnp.repeat(widened, block_size, axis=2)


def slot_table(picked, rounded, flight, capacity):
    token_count, pick_count = picked.shape
    flattened = picked.reshape(-1)
    matches = (flattened[:, None] == jnp.arange(flight, dtype=jnp.int32)[None, :]).astype(jnp.int32)
    before = jnp.cumsum(matches, axis=0) - matches
    slot_rank = jnp.sum(before * matches, axis=1)
    in_window = flattened < flight
    target = jnp.where(in_window, flattened * capacity + slot_rank, flight * capacity)
    source_row = jnp.arange(token_count * pick_count, dtype=jnp.int32) // pick_count
    token_of = jnp.full((flight * capacity,), -1, jnp.int32).at[target].set(source_row, mode="drop")
    weight_of = (
        jnp.zeros((flight * capacity,), rounded.dtype)
        .at[target]
        .set(rounded.reshape(-1), mode="drop")
    )
    return (token_of, weight_of)


def activate(totals, scaling):
    factor = scaling.astype(jnp.float32)[..., None]
    return (factor * jax.nn.silu(totals[0]) * totals[1]).astype(jnp.bfloat16)


def shards(tokens, route_ids, route_weight, gate_up, block_keep):
    flight = lax.axis_size("expert")
    capacity = CAP
    masked = gate_up[0] * expand_mask(block_keep[0], BLOCK).astype(gate_up.dtype)
    hidden_units = masked.shape[2]
    rounded = route_weight.astype(jnp.bfloat16)
    token_of, weight_of = slot_table(route_ids, rounded, flight, capacity)
    filled = (token_of >= 0)[:, None]
    clipped = jnp.maximum(token_of, 0)
    slot_weight = weight_of.reshape(flight, capacity)
    gathered = lax.all_gather(tokens, "tensor", axis=1, tiled=True)
    picked_rows = jnp.where(
        filled, jnp.take(gathered, clipped, axis=0), jnp.zeros((), gathered.dtype)
    )
    outgoing = picked_rows.reshape(flight, capacity, gathered.shape[1])
    arrived = lax.all_to_all(outgoing, "expert", split_axis=0, concat_axis=0, tiled=True)
    scaling = lax.all_to_all(slot_weight, "expert", split_axis=0, concat_axis=0, tiled=True)
    totals = jnp.einsum("scd,kdf->kscf", arrived, masked, preferred_element_type=jnp.float32)
    hidden = activate(totals, scaling)
    hidden = hidden.reshape(1, -1, hidden_units)
    return hidden


def solution(mesh):
    return jax.shard_map(
        shards,
        mesh=mesh,
        in_specs=(
            P("expert", "tensor"),
            P("expert", None),
            P("expert", None),
            P("expert", None, None, "tensor"),
            P("expert", None, None, "tensor"),
        ),
        out_specs=P("expert", None, "tensor"),
        check_vma=False,
    )
```

profile of v0, /device:TPU:11, one launch (start us, length us, event | category | flops | bytes accessed | tf_op | source)
XLA Modules:
  0.0 113.2 jit_solution(4909169843594489254)
XLA Ops:
  6.5 0.0 all-gather.2.cloned.1.call-start
  6.5 0.7 all-gather.2.cloned.1.call-update
  7.3 0.8 copy.41
  8.0 0.1 eq.29
  8.1 0.1 eq.25
  8.2 0.7 convert_element_type.46
  8.9 0.7 broadcast_compare_fusion
  9.6 0.1 copy.39
  9.7 0.1 lt.33
  9.8 0.1 copy.45
  10.0 0.1 reshape.171
  10.1 0.7 broadcast_multiply_fusion
  10.8 0.1 copy.40
  10.9 0.1 mul.60
  11.0 4.5 %reduce-window.6 = s32[16,8,128]{2,1,0:T(8,128)S(1)} reduce-window(s32[16,8,128]{2,1,0:T(8,128)S(1)} %fusion.18, s32[]{:T(128)} %constant.46.clone.1), window={size=1x1x128 pad=0_0x0_0x127_0}, to_apply=%region_0.0 | reduce-window | flops 2080768 | bytes 131076 | tf_op jit(solution)/shard_map/reduce-window
  15.5 0.1 slice.18
  15.6 0.1 copy.43
  15.8 0.1 copy.44
  15.8 0.1 broadcast_add_fusion
  16.0 7.6 %scatter_custom_fusion = bf16[128]{0:T(256)(128)(2,1)S(1)} fusion(s32[1024]{0:T(1024)S(1)} %bitcast.72, bf16[1024]{0:T(1024)(128)(2,1)S(1)} %reshape.171, bf16[]{:T(256)} %constant.43.clone.1), kind=kCustom, calls=%fused_computation.45 | custom fusion | bytes 258 | tf_op jit(solution)/shard_map/scatter | solution.py:28
  23.6 0.7 all_to_all.12
  24.3 6.6 %all-to-all-start = ((bf16[16,1,8]{2,1,0:T(2,128)(2,1)}), bf16[16,1,8]{2,1,0:T(2,128)(2,1)S(1)}, u32[]{:S(2)}, u32[]{:S(2)}) async-start(bf16[16,1,8]{2,1,0:T(2,128)(2,1)} %all_to_all.12), calls=%async_computation | async-start | bytes 16384 | tf_op jit(solution)/shard_map/all_to_all | solution.py:54
  30.8 4.3 %scatter_custom_fusion.1 = s32[128]{0:T(128)S(1)} fusion(s32[1024]{0:T(1024)S(1)} %bitcast.73, s32[1024]{0:T(1024)S(1)} %add_select_fusion, s32[]{:T(128)} %constant.48.clone.1), kind=kCustom, calls=%fused_computation.43 | custom fusion | bytes 516 | tf_op jit(solution)/shard_map/scatter | solution.py:24
  35.1 0.1 broadcast_in_dim.54
  35.2 0.1 broadcast_in_dim.56
  35.4 4.9 %all-gather.2.cloned.1.call-done = bf16[128,7168]{1,0:T(8,128)(2,1)} async-done(((bf16[128,3584]{1,0:T(8,128)(2,1)}), bf16[128,7168]{1,0:T(8,128)(2,1)}) %all-gather.2.cloned.1.call-update) | async-done | bytes 1835024 | tf_op jit(solution)/shard_map/all_gather | solution.py:48
  40.2 5.1 %gather_fusion = bf16[128,7168]{1,0:T(8,128)(2,1)S(1)} fusion(bf16[128,7168]{1,0:T(8,128)(2,1)} %all-gather.2.cloned.1.call-done, s32[1024]{0:T(1024)S(1)} %pad_clamp_fusion), kind=kCustom, calls=%fused_computation | custom fusion | bytes 3670528 | tf_op jit(solution)/shard_map/jit(_take)/gather | solution.py:50
  45.3 1.5 %fusion.3 = bf16[16,8,7168]{2,1,0:T(8,128)(2,1)} fusion(bf16[128,7168]{1,0:T(8,128)(2,1)S(1)} %gather_fusion, pred[16,8]{1,0:T(8,128)(4,1)S(1)} %broadcast_in_dim.56, pred[16,8]{1,0:T(8,128)(4,1)S(1)} %broadcast_in_dim.54), kind=kLoop, calls=%fused_computation.8 | loop fusion | flops 1835008 | bytes 3670272 | tf_op jit(solution)/shard_map/jit(_where)/select_n | solution.py:49
  46.9 0.0 copy-start
  46.9 0.0 all-to-all-done
  46.9 6.5 %all-to-all-start.1 = ((bf16[16,8,7168]{2,1,0:T(8,128)(2,1)}), bf16[16,8,7168]{2,1,0:T(8,128)(2,1)S(1)}, u32[]{:S(2)}, u32[]{:S(2)}) async-start(bf16[16,8,7168]{2,1,0:T(8,128)(2,1)} %fusion.3), calls=%async_computation.1 | async-start | bytes 3670016 | tf_op jit(solution)/shard_map/all_to_all | solution.py:53
  53.4 0.0 copy-done
  53.4 0.3 broadcast_in_dim.51
  53.7 0.3 convert_element_type.51
  54.0 18.8 %copy.47 = bf16[1,2,7168,512]{2,3,1,0:T(8,128)(2,1)} copy(bf16[1,2,7168,512]{3,2,1,0:T(8,128)(2,1)} %param.8) | data formatting | bytes 29360128 | tf_op args[3]
  72.8 13.2 %bitcast_multiply_fusion = bf16[2,7168,512]{1,2,0:T(8,128)(2,1)} fusion(bf16[1,2,7168,512]{2,3,1,0:T(8,128)(2,1)} %copy.47, bf16[2,7168,8]{1,2,0:T(8,128)(2,1)S(1)} %convert_element_type.51), kind=kLoop, calls=%fused_computation.5 | loop fusion | flops 7340032 | bytes 29589504 | tf_op jit(solution)/shard_map/mul | solution.py:41
  86.1 0.1 reshape.158
  86.1 9.0 %all-to-all-done.1 = bf16[16,8,7168]{2,1,0:T(8,128)(2,1)S(1)} async-done(((bf16[16,8,7168]{2,1,0:T(8,128)(2,1)}), bf16[16,8,7168]{2,1,0:T(8,128)(2,1)S(1)}, u32[]{:S(2)}, u32[]{:S(2)}) %all-to-all-start.1) | async-done | bytes 1835040 | tf_op jit(solution)/shard_map/all_to_all | solution.py:53
  95.2 10.2 %fusion.5 = f32[2,16,8,512]{3,1,2,0:T(8,128)S(1)} fusion(bf16[16,8,7168]{2,1,0:T(8,128)(2,1)S(1)} %all-to-all-done.1, bf16[2,7168,512]{1,2,0:T(8,128)(2,1)} %bitcast_multiply_fusion), kind=kOutput, calls=%fused_computation.10 | convolution fusion | flops 1879048192 | bytes 17039360 | tf_op jit(solution)/shard_map/scd,kdf->kscf/dot_general | solution.py:55
  105.4 1.0 fusion.10
  (12 shorter events, 0.2 us)
Async XLA Ops:
  6.5 33.7 %all-gather.2.cloned.1.call-start = ((), (), s32[]{:S(2)}) async-start(), calls=%async_computation.2 | async-start | bytes 2752512 | tf_op jit(solution)/shard_map/all_gather | solution.py:48
  24.3 22.6 %all-to-all-start = ((bf16[16,1,8]{2,1,0:T(2,128)(2,1)}), bf16[16,1,8]{2,1,0:T(2,128)(2,1)S(1)}, u32[]{:S(2)}, u32[]{:S(2)}) async-start(bf16[16,1,8]{2,1,0:T(2,128)(2,1)} %all_to_all.12), calls=%async_computation | async-start | bytes 16384 | tf_op jit(solution)/shard_map/all_to_all | solution.py:54
  46.9 6.5 %copy-start = (s32[1,2,112,8]{2,3,1,0:T(8,128)S(1)}, s32[1,2,112,8]{2,3,1,0:T(8,128)}, u32[]{:S(2)}) copy-start(s32[1,2,112,8]{2,3,1,0:T(8,128)} %param.9) | copy-start | bytes 21508
  46.9 48.3 %all-to-all-start.1 = ((bf16[16,8,7168]{2,1,0:T(8,128)(2,1)}), bf16[16,8,7168]{2,1,0:T(8,128)(2,1)S(1)}, u32[]{:S(2)}, u32[]{:S(2)}) async-start(bf16[16,8,7168]{2,1,0:T(8,128)(2,1)} %fusion.3), calls=%async_computation.1 | async-start | bytes 3670016 | tf_op jit(solution)/shard_map/all_to_all | solution.py:53
Sparse Core Ops, SparseCore 0:
  8.9 31.2 all-gather.1
where the time goes:
time: 114 us; the launch traced here: 113 us
  local copies, waits for them, and re-layouts  39.3 us (34%)
  other arithmetic  22.5 us (20%)
  waiting for transfers between devices  14.6 us (13%)
  between operations  13.5 us (12%)
  starting transfers between devices  13.1 us (11%)
  matrix products  10.2 us (9%)
    unnamed x4, local copies, waits for them, and re-layouts  19.6 us
    mul x1, other arithmetic, shards(): gate_up[0] * expand_mask(block_keep[0], BLOCK).astype(gate_up.dtype)  13.2 us
    dot_general x1, matrix products, shards(): jnp.einsum('scd,kdf->kscf', arrived, masked, preferred_element_type=jnp.f...  10.2 us
    all_to_all x1, waiting for transfers between devices, shards(): lax.all_to_all(outgoing, 'expert', split_axis=0, concat_axis=0, tiled=True)  9.03 us
    scatter x1, local copies, waits for them, and re-layouts, slot_table(): weight_of = jnp.zeros((flight * capacity,), rounded.dtype).at[target].set...  7.58 us
    all_to_all x1, starting transfers between devices, shards(): lax.all_to_all(slot_weight, 'expert', split_axis=0, concat_axis=0, tiled=...  6.55 us
    all_to_all x1, starting transfers between devices, shards(): lax.all_to_all(outgoing, 'expert', split_axis=0, concat_axis=0, tiled=True)  6.51 us
    gather x1, local copies, waits for them, and re-layouts, shards(): jnp.take(gathered, clipped, axis=0)  5.1 us
  transfers between devices with their start and end apart: 3, of which 2 were waited for; matrix products, arithmetic and copies ran while one was open for 53% of the time, Pallas kernels for 0%

commit v1 on v0

--- a/solution.py
+++ b/solution.py
@@ -1,10 +1,16 @@
+import functools
+
 import jax
 import jax.numpy as jnp
 from jax import lax
+from jax.experimental import pallas as pl
+from jax.experimental.pallas import tpu as pltpu
 from jax.sharding import PartitionSpec as P
 
 BLOCK = 64
 CAP = 8
+LANES = 128
+PAIR = 2 * CAP
 
 
 def expand_mask(keep_mask, block_size):
@@ -35,32 +41,287 @@
     return (factor * jax.nn.silu(totals[0]) * totals[1]).astype(jnp.bfloat16)
 
 
-def shards(tokens, route_ids, route_weight, gate_up, block_keep):
+def gathered_form(tokens, route_ids, route_weight, gate_up, block_keep):
     flight = lax.axis_size("expert")
-    capacity = CAP
     masked = gate_up[0] * expand_mask(block_keep[0], BLOCK).astype(gate_up.dtype)
     hidden_units = masked.shape[2]
     rounded = route_weight.astype(jnp.bfloat16)
-    token_of, weight_of = slot_table(route_ids, rounded, flight, capacity)
+    token_of, weight_of = slot_table(route_ids, rounded, flight, CAP)
     filled = (token_of >= 0)[:, None]
-    clipped = jnp.maximum(token_of, 0)
-    slot_weight = weight_of.reshape(flight, capacity)
-    gathered = lax.all_gather(tokens, "tensor", axis=1, tiled=True)
     picked_rows = jnp.where(
-        filled, jnp.take(gathered, clipped, axis=0), jnp.zeros((), gathered.dtype)
-    )
-    outgoing = picked_rows.reshape(flight, capacity, gathered.shape[1])
+        filled, jnp.take(tokens, jnp.maximum(token_of, 0), axis=0), jnp.zeros((), tokens.dtype)
+    )
+    outgoing = picked_rows.reshape(flight, CAP, tokens.shape[1])
     arrived = lax.all_to_all(outgoing, "expert", split_axis=0, concat_axis=0, tiled=True)
-    scaling = lax.all_to_all(slot_weight, "expert", split_axis=0, concat_axis=0, tiled=True)
+    scaling = lax.all_to_all(
+        weight_of.reshape(flight, CAP), "expert", split_axis=0, concat_axis=0, tiled=True
+    )
+    arrived = lax.all_gather(arrived, "tensor", axis=2, tiled=True)
     totals = jnp.einsum("scd,kdf->kscf", arrived, masked, preferred_element_type=jnp.float32)
-    hidden = activate(totals, scaling)
-    hidden = hidden.reshape(1, -1, hidden_units)
-    return hidden
+    return activate(totals, scaling).reshape(1, -1, hidden_units)
+
+
+def chosen_rows(groups, place, block, ids, wgt):
+    chip, core = place[0] // 2, lax.rem(place[0], 2)
+    count = ids.shape[1]
+    rows = lax.broadcasted_iota(jnp.int32, (count, count), 0)
+    cols = lax.broadcasted_iota(jnp.int32, (count, count), 1)
+    earlier = (rows < cols).astype(jnp.bfloat16)
+    slot = lax.broadcasted_iota(jnp.int32, (PAIR, count), 0)
+    rank_wanted = lax.rem(slot, CAP).astype(jnp.float32)
+    here = slot // CAP == core ^ block
+    rounded = wgt.astype(jnp.bfloat16).astype(jnp.float32)
+    named, scale = [], []
+    for k in range(groups):
+        hit = ids == 2 * (chip ^ k) + core
+        named.append(jnp.sum(hit.astype(jnp.float32), axis=0, keepdims=True))
+        scale.append(jnp.sum(jnp.where(hit, rounded, 0.0), axis=0, keepdims=True))
+    before = jnp.dot(
+        jnp.concatenate(named, axis=0).astype(jnp.bfloat16), earlier, preferred_element_type=jnp.float32
+    )
+    chosen, weights = [], []
+    for k in range(groups):
+        pick = here & (named[k] > 0.5) & (before[k : k + 1] == rank_wanted)
+        chosen.append(pick.astype(jnp.float32))
+        weights.append(jnp.sum(chosen[k] * scale[k], axis=1, keepdims=True))
+    return jnp.concatenate(chosen, axis=0).astype(jnp.bfloat16), jnp.concatenate(weights, axis=0)
+
+
+def spans(width):
+    step = next(s for s in (512, 384, 256, 128) if width % s == 0)
+    return [slice(at, at + step) for at in range(0, width, step)]
+
+
+def own_kernel(groups, place, ids_hbm, wgt_hbm, tok_hbm, out_ref, ids_ref, wgt_ref, tok_ref, sems):
+    copies = [
+        pltpu.make_async_copy(a, b, sems.at[i])
+        for i, (a, b) in enumerate(((ids_hbm, ids_ref), (wgt_hbm, wgt_ref), (tok_hbm, tok_ref)))
+    ]
+    for copy in copies:
+        copy.start()
+    copies[0].wait()
+    copies[1].wait()
+    picks, weights = chosen_rows(groups, place, 0, ids_ref[...], wgt_ref[...])
+    width = tok_ref.shape[1]
+    copies[2].wait()
+    for span in spans(width):
+        got = jnp.dot(picks, tok_ref[:, span], preferred_element_type=jnp.float32)
+        out_ref[:, span] = got.astype(out_ref.dtype)
+    out_ref[:, width:] = jnp.broadcast_to(weights, (weights.shape[0], LANES)).astype(out_ref.dtype)
+
+
+def pair_kernel(groups, near, place, ids_ref, wgt_ref, tok_ref, own_ref, near_ref, *far_refs):
+    picks, weights = chosen_rows(groups, place, 1, ids_ref[...], wgt_ref[...])
+    width = tok_ref.shape[1]
+
+    def put(span, got):
+        got = (got + own_ref[:, span].astype(jnp.float32)).astype(near_ref.dtype)
+        near_ref[:, span] = got[: PAIR * near]
+        for k, far_ref in enumerate(far_refs):
+            far_ref[:, span] = got[PAIR * (near + k) : PAIR * (near + k + 1)]
+
+    for span in spans(width):
+        put(span, jnp.dot(picks, tok_ref[:, span], preferred_element_type=jnp.float32))
+    put(slice(width, width + LANES), jnp.broadcast_to(weights, (weights.shape[0], LANES)))
+
+
+def dispatch(place, ids, wgt, tok, partner, groups, near):
+    count, width = tok.shape
+    smem = pl.BlockSpec(memory_space=pltpu.SMEM)
+    vmem = pl.BlockSpec(memory_space=pltpu.VMEM)
+    hbm = pl.BlockSpec(memory_space=pl.ANY)
+    cost = pl.CostEstimate(
+        flops=2 * PAIR * groups * count * width, bytes_accessed=2 * count * width, transcendentals=0
+    )
+    own = pl.pallas_call(
+        functools.partial(own_kernel, groups),
+        out_shape=jax.ShapeDtypeStruct((PAIR * groups, width + LANES), tok.dtype),
+        in_specs=[smem, hbm, hbm, hbm],
+        out_specs=vmem,
+        scratch_shapes=[pltpu.VMEM(a.shape, a.dtype) for a in (ids, wgt, tok)] + [pltpu.SemaphoreType.DMA((3,))],
+        compiler_params=pltpu.CompilerParams(vmem_limit_bytes=16 << 20),
+        cost_estimate=cost,
+        name="own_rows",
+    )(place, *(pltpu.with_memory_space_constraint(a, pltpu.HBM) for a in (ids, wgt, tok)))
+    shapes = [jax.ShapeDtypeStruct((PAIR * near, width + LANES), tok.dtype)]
+    shapes += [jax.ShapeDtypeStruct((PAIR, width + LANES), tok.dtype)] * (groups - near)
+    return pl.pallas_call(
+        functools.partial(pair_kernel, groups, near),
+        out_shape=shapes,
+        in_specs=[smem] + [vmem] * 4,
+        out_specs=[vmem] * len(shapes),
+        compiler_params=pltpu.CompilerParams(vmem_limit_bytes=16 << 20),
+        cost_estimate=cost,
+        name="pair_rows",
+    )(place, *partner, own)
+
+
+def mask_kernel(keep_ref, mat_hbm, out_ref, mask_ref, sems):
+    parts = sems.shape[1]
+    units, depth = out_ref.shape[2], out_ref.shape[1] // parts
+    copies = [
+        [
+            pltpu.make_async_copy(
+                mat_hbm.at[m, pl.ds(p * depth, depth)], out_ref.at[m, pl.ds(p * depth, depth)], sems.at[m, p]
+            )
+            for p in range(parts)
+        ]
+        for m in range(2)
+    ]
+    for p in range(parts):
+        for m in range(2):
+            copies[m][p].start()
+    cols = keep_ref.shape[1]
+    lane = lax.broadcasted_iota(jnp.int32, (cols, units), 1) // BLOCK
+    row = lax.broadcasted_iota(jnp.int32, (cols, units), 0)
+    widen = (lane == row).astype(jnp.bfloat16)
+    for m in range(2):
+        mask_ref[m] = lax.dot_general(
+            keep_ref[m].astype(jnp.float32).astype(jnp.bfloat16),
+            widen,
+            (((0,), (0,)), ((), ())),
+            preferred_element_type=jnp.float32,
+        )
+    for p in range(parts):
+        for m in range(2):
+            copies[m][p].wait()
+
+            @pl.loop(0, depth // BLOCK)
+            def _(r):
+                at = p * (depth // BLOCK) + r
+                keep = mask_ref[m, pl.ds(at, 1), :].astype(out_ref.dtype)
+                span = pl.ds(pl.multiple_of(at * BLOCK, BLOCK), BLOCK)
+                out_ref[m, span, :] = out_ref[m, span, :] * keep
+
+
+def mask_matrices(keep, matrices):
+    rows, units = matrices.shape[1:]
+    parts = next(p for p in (14, 16, 8, 7, 4, 2, 1) if rows % (p * BLOCK) == 0)
+    vmem = pl.BlockSpec(memory_space=pltpu.VMEM)
+    return pl.pallas_call(
+        mask_kernel,
+        out_shape=jax.ShapeDtypeStruct(matrices.shape, matrices.dtype),
+        in_specs=[vmem, pl.BlockSpec(memory_space=pl.ANY)],
+        out_specs=vmem,
+        scratch_shapes=[pltpu.VMEM((2, rows // BLOCK, units), jnp.float32), pltpu.SemaphoreType.DMA((2, parts))],
+        compiler_params=pltpu.CompilerParams(vmem_limit_bytes=20 << 20),
+        cost_estimate=pl.CostEstimate(flops=2 * rows * units, bytes_accessed=4 * rows * units, transcendentals=0),
+        name="mask_matrices",
+    )(keep, pltpu.with_memory_space_constraint(matrices, pltpu.HBM))
+
+
+def join_kernel(near, own_ref, other_ref, *out_refs):
+    for k, out_ref in enumerate(out_refs):
+        span = slice(PAIR * (k + 1), PAIR * (k + 2))
+        out_ref[:PAIR] = own_ref[span]
+        out_ref[PAIR:] = other_ref[span]
+
+
+def join(own, other, near):
+    vmem = pl.BlockSpec(memory_space=pltpu.VMEM)
+    return pl.pallas_call(
+        functools.partial(join_kernel, near),
+        out_shape=[jax.ShapeDtypeStruct((2 * PAIR, own.shape[1]), own.dtype)] * (near - 1),
+        in_specs=[vmem] * 2,
+        out_specs=[vmem] * (near - 1),
+        compiler_params=pltpu.CompilerParams(vmem_limit_bytes=4 << 20),
+        name="join",
+    )(own, other)
+
+
+def project_kernel(groups, near, last, place, mat_ref, *refs):
+    pieces, refs = refs[:groups], refs[groups:]
+    if last:
+        total_ref, scale_ref, out_ref, x_ref = refs
+    else:
+        total_ref, scale_ref, x_ref = refs
+    chip = place[0] // 2
+    width = x_ref.shape[1]
+    for k in range(groups):
+        at = pl.multiple_of(PAIR * (chip ^ k), PAIR)
+        half = slice(PAIR, None) if last and 0 < k < near else slice(0, PAIR)
+        x_ref[pl.ds(at, PAIR), :] = pieces[k][half, :width]
+        if not last:
+            scale_ref[pl.ds(at, PAIR), :] = pieces[k][:PAIR, width:].astype(jnp.float32)
+    share = 1 - place[1] if last else place[1]
+    span = pl.ds(pl.multiple_of(share * width, BLOCK), width)
+    totals = [jnp.dot(x_ref[...], mat_ref[m, span, :], preferred_element_type=jnp.float32) for m in range(2)]
+    if last:
+        gate, up = (total_ref[m] + totals[m] for m in range(2))
+        out_ref[0] = (scale_ref[:, :1] * (gate / (1.0 + jnp.exp(-gate))) * up).astype(out_ref.dtype)
+    else:
+        for m in range(2):
+            total_ref[m] = totals[m]
+
+
+def project(place, matrices, pieces, groups, near, width, total=None, scale=None):
+    last = total is not None
+    units = matrices.shape[2]
+    slots = PAIR * groups
+    vmem = pl.BlockSpec(memory_space=pltpu.VMEM)
+    args = [place, matrices, *pieces]
+    if last:
+        args += [total, scale]
+        out_shape = jax.ShapeDtypeStruct((1, slots, units), jnp.bfloat16)
+    else:
+        out_shape = [
+            jax.ShapeDtypeStruct((2, slots, units), jnp.float32),
+            jax.ShapeDtypeStruct((slots, LANES), jnp.float32),
+        ]
+    return pl.pallas_call(
+        functools.partial(project_kernel, groups, near, last),
+        out_shape=out_shape,
+        in_specs=[pl.BlockSpec(memory_space=pltpu.SMEM)] + [vmem] * (len(args) - 1),
+        out_specs=vmem if last else [vmem, vmem],
+        scratch_shapes=[pltpu.VMEM((slots, width), jnp.bfloat16)],
+        compiler_params=pltpu.CompilerParams(vmem_limit_bytes=24 << 20),
+        cost_estimate=pl.CostEstimate(
+            flops=4 * slots * width * units, bytes_accessed=4 * width * units, transcendentals=slots * units
+        ),
+        name="project_last" if last else "project_first",
+    )(*args)
+
+
+def paired_form(tokens, route_ids, route_weight, gate_up, block_keep):
+    n = lax.axis_size("expert")
+    groups = n // 2
+    near = groups // 2
+    me = lax.axis_index("expert")
+    place = jnp.stack([me, lax.axis_index("tensor")]).astype(jnp.int32)
+    width = tokens.shape[1]
+
+    def move(a, shift):
+        return lax.ppermute(a, "expert", [(s, s ^ shift) for s in range(n)])
+
+    def cross(a):
+        return lax.ppermute(a, "tensor", [(0, 1), (1, 0)])
+
+    ids, wgt = route_ids.T, route_weight.T
+    partner = [move(a, 1) for a in (ids, wgt, tokens)]
+    own, *far = dispatch(place, ids, wgt, tokens, partner, groups, near)
+    keep = jnp.swapaxes(block_keep[0], 1, 2)
+    keep, own = lax.optimization_barrier((keep, own))
+    masked = mask_matrices(keep, gate_up[0])
+    far_order = sorted(range(groups - near), key=lambda k: (k % 2, -k))
+    far_in = [None] * (groups - near)
+    for k in far_order:
+        far_in[k] = move(far[k], 2 * (near + k))
+    other, masked = lax.optimization_barrier((cross(own), masked))
+    both = join(own, other, near)
+    near_in = [move(b, 2 * (k + 1)) for k, b in enumerate(both)]
+    far_other = [None] * (groups - near)
+    for k in far_order:
+        far_other[k] = cross(far_in[k])
+
+    total, scale = project(place, masked, [own, *near_in, *far_in], groups, near, width)
+    return project(place, masked, [other, *near_in, *far_other], groups, near, width, total, scale)
 
 
 def solution(mesh):
+    shares, experts = mesh.shape["tensor"], mesh.shape["expert"]
+    paired = shares == 2 and 8 <= experts <= 16 and experts & (experts - 1) == 0
     return jax.shard_map(
-        shards,
+        paired_form if paired else gathered_form,
         mesh=mesh,
         in_specs=(
             P("expert", "tensor"),

time: 114 us -> 49.9 us (0.44)
  the two profiles are of different devices: /device:TPU:11 before, /device:TPU:0 now
where the time goes in v1:
time: 49.9 us; the launch traced here: 49.1 us
  starting transfers between devices  20.7 us (41%)
  waiting for transfers between devices  14.6 us (29%)
  Pallas kernels  12.9 us (26%)
  local copies, waits for them, and re-layouts  0.7 us (1%)
    ppermute x10, starting transfers between devices, move(): return lax.ppermute(a, 'expert', [(s, s ^ shift) for s in range(n)])  13.3 us
    ppermute x10, waiting for transfers between devices, move(): return lax.ppermute(a, 'expert', [(s, s ^ shift) for s in range(n)])  9.3 us
    ppermute x5, starting transfers between devices, cross(): return lax.ppermute(a, 'tensor', [(0, 1), (1, 0)])  7.39 us
    pallas_call x1, Pallas kernels, mask_matrices(): pl.pallas_call(mask_kernel, out_shape=jax.ShapeDtypeStruct(matrices.shape...  5.51 us
    ppermute x5, waiting for transfers between devices, cross(): return lax.ppermute(a, 'tensor', [(0, 1), (1, 0)])  5.33 us
    pallas_call x2, Pallas kernels, project(): pl.pallas_call(functools.partial(project_kernel, groups, near, last), out...  4.07 us
    pallas_call x1, Pallas kernels, dispatch(): pl.pallas_call(functools.partial(own_kernel, groups), out_shape=jax.Shape...  2.17 us
    pallas_call x1, Pallas kernels, dispatch(): pl.pallas_call(functools.partial(pair_kernel, groups, near), out_shape=sh...  1.07 us
  transfers between devices with their start and end apart: 15, of which 5 were waited for; matrix products, arithmetic and copies ran while one was open for 0% of the time, Pallas kernels for 19%

profile of v1, /device:TPU:0, one launch (start us, length us, event | category | flops | bytes accessed | tf_op | source)
XLA Modules:
  0.0 49.1 jit_solution(15507554892456581127)
XLA Ops:
  0.0 0.5 collective-permute-start.2
  0.5 0.1 collective-permute-start
  0.5 0.5 collective-permute-start.1
  1.0 0.1 pad_add_fusion.place
  1.0 2.2 %own_rows.1.own_ref = bf16[128,3712]{1,0:T(8,128)(2,1)S(1)} custom-call(s32[2]{0:T(128)S(1)} %pad_add_fusion.place, s32[8,128]{1,0:T(8,128)} %bitcast.11, f32[8,128]{1,0:T(8,128)} %bitcast.13, bf16[128,3584]{1,0:T(8,128)(2,1)} %tok_hbm.1), custom_call_target="tpu_custom_call" | custom-call | flops 117440512 | bytes 917504 | tf_op jit(solution)/shard_map/own_rows/pallas_call | solution.py:136
  3.2 0.0 collective-permute-done.ids_ref
  3.2 0.0 collective-permute-done.1.wgt_ref
  3.2 0.0 collective-permute-done.2.tok_ref
  3.3 1.1 %pair_rows.1 = (bf16[64,3712]{1,0:T(8,128)(2,1)S(1)}, bf16[16,3712]{1,0:T(8,128)(2,1)S(1)}, bf16[16,3712]{1,0:T(8,128)(2,1)S(1)}, bf16[16,3712]{1,0:T(8,128)(2,1)S(1)}, bf16[16,3712]{1,0:T(8,128)(2,1)S(1)}) custom-call(s32[2]{0:T(128)S(1)} %pad_add_fusion.place, s32[8,128]{1,0:T(8,128)S(1)} %collective-permute-done.ids_ref, ...), custom_call_target="tpu_custom_call" | custom-call | flops 117440512 | bytes 917504 | tf_op jit(solution)/shard_map/pair_rows/pallas_call | solution.py:148
  4.3 2.6 %collective-permute-start.3 = (bf16[64,3712]{1,0:T(8,128)(2,1)S(1)}, bf16[64,3712]{1,0:T(8,128)(2,1)S(1)}, u32[]{:S(2)}, u32[]{:S(2)}) collective-permute-start(bf16[64,3712]{1,0:T(8,128)(2,1)S(1)} %get-tuple-element.20.own_ref.refs_0_), channel_id=1, source_target_pairs={{0,1},{1,0},{2,3},{3,2},{4,5},{5,4},{6,7},{7,6},{8,9},{9,8},{10,11... | collective-permute-start | bytes 1425416 | tf_op jit(solution)/shard_map/ppermute | solution.py:297
  6.9 3.6 %collective-permute-start.11 = (bf16[16,3712]{1,0:T(8,128)(2,1)S(1)}, bf16[16,3712]{1,0:T(8,128)(2,1)S(1)}, u32[]{:S(2)}, u32[]{:S(2)}) collective-permute-start(bf16[16,3712]{1,0:T(8,128)(2,1)S(1)} %get-tuple-element.29), channel_id=1, source_target_pairs={{0,24},{2,26},{4,28},{6,30},{8,16},{10,18},{12,20},{14,22},{16,8},... | collective-permute-start | bytes 356360 | tf_op jit(solution)/shard_map/ppermute | solution.py:294
  10.5 1.2 %collective-permute-start.13 = (bf16[16,3712]{1,0:T(8,128)(2,1)S(1)}, bf16[16,3712]{1,0:T(8,128)(2,1)S(1)}, u32[]{:S(2)}, u32[]{:S(2)}) collective-permute-start(bf16[16,3712]{1,0:T(8,128)(2,1)S(1)} %get-tuple-element.30), channel_id=1, source_target_pairs={{0,28},{2,30},{4,24},{6,26},{8,20},{10,22},{12,16},{14,18},{16,12}... | collective-permute-start | bytes 356360 | tf_op jit(solution)/shard_map/ppermute | solution.py:294
  11.7 0.0 copy-start
  11.7 0.7 %copy-done = s32[1,2,112,8]{2,3,1,0:T(8,128)S(1)} copy-done((s32[1,2,112,8]{2,3,1,0:T(8,128)S(1)}, s32[1,2,112,8]{2,3,1,0:T(8,128)}, u32[]{:S(2)}) %copy-start) | copy-done | bytes 7192
  12.4 5.5 %mask_matrices.1.mat_ref = bf16[2,7168,512]{2,1,0:T(8,128)(2,1)S(1)} custom-call(s32[2,8,112]{2,1,0:T(8,128)S(1)} %bitcast.8, bf16[2,7168,512]{2,1,0:T(8,128)(2,1)} %bitcast.9), custom_call_target="tpu_custom_call" | custom-call | flops 7340032 | bytes 14680064 | tf_op jit(solution)/shard_map/mask_matrices/pallas_call | solution.py:201
  17.9 0.6 %collective-permute-done.3.other_ref.refs_0_ = bf16[64,3712]{1,0:T(8,128)(2,1)S(1)} collective-permute-done((bf16[64,3712]{1,0:T(8,128)(2,1)S(1)}, bf16[64,3712]{1,0:T(8,128)(2,1)S(1)}, u32[]{:S(2)}, u32[]{:S(2)}) %collective-permute-start.3) | collective-permute-done | bytes 475168 | tf_op jit(solution)/shard_map/ppermute | solution.py:297
  18.5 1.8 %collective-permute-start.4 = (bf16[32,3712]{1,0:T(8,128)(2,1)S(1)}, bf16[32,3712]{1,0:T(8,128)(2,1)S(1)}, u32[]{:S(2)}, u32[]{:S(2)}) collective-permute-start(bf16[32,3712]{1,0:T(8,128)(2,1)S(1)} %get-tuple-element.24), channel_id=1, source_target_pairs={{0,4},{2,6},{4,0},{6,2},{8,12},{10,14},{12,8},{14,10},{16,20},{18,... | collective-permute-start | bytes 712712 | tf_op jit(solution)/shard_map/ppermute | solution.py:294
  20.3 1.6 %collective-permute-start.5 = (bf16[32,3712]{1,0:T(8,128)(2,1)S(1)}, bf16[32,3712]{1,0:T(8,128)(2,1)S(1)}, u32[]{:S(2)}, u32[]{:S(2)}) collective-permute-start(bf16[32,3712]{1,0:T(8,128)(2,1)S(1)} %get-tuple-element.25), channel_id=1, source_target_pairs={{0,8},{2,10},{4,12},{6,14},{8,0},{10,2},{12,4},{14,6},{16,24},{18,... | collective-permute-start | bytes 712712 | tf_op jit(solution)/shard_map/ppermute | solution.py:294
  21.9 0.2 collective-permute-start.6
  22.1 0.0 collective-permute-done.11.refs_6_
  22.1 3.8 %collective-permute-start.9 = (bf16[16,3712]{1,0:T(8,128)(2,1)S(1)}, bf16[16,3712]{1,0:T(8,128)(2,1)S(1)}, u32[]{:S(2)}, u32[]{:S(2)}) collective-permute-start(bf16[16,3712]{1,0:T(8,128)(2,1)S(1)} %get-tuple-element.28), channel_id=1, source_target_pairs={{0,20},{2,22},{4,16},{6,18},{8,28},{10,30},{12,24},{14,26},{16,4},... | collective-permute-start | bytes 356360 | tf_op jit(solution)/shard_map/ppermute | solution.py:294
  25.8 0.0 collective-permute-done.13.refs_7_
  25.8 0.3 collective-permute-start.7
  26.1 9.3 %collective-permute-done.9.refs_5_ = bf16[16,3712]{1,0:T(8,128)(2,1)S(1)} collective-permute-done((bf16[16,3712]{1,0:T(8,128)(2,1)S(1)}, bf16[16,3712]{1,0:T(8,128)(2,1)S(1)}, u32[]{:S(2)}, u32[]{:S(2)}) %collective-permute-start.9) | collective-permute-done | bytes 118816 | tf_op jit(solution)/shard_map/ppermute | solution.py:294
  35.4 1.5 %collective-permute-start.10 = (bf16[16,3712]{1,0:T(8,128)(2,1)S(1)}, bf16[16,3712]{1,0:T(8,128)(2,1)S(1)}, u32[]{:S(2)}, u32[]{:S(2)}) collective-permute-start(bf16[16,3712]{1,0:T(8,128)(2,1)S(1)} %collective-permute-done.9.refs_5_), channel_id=1, source_target_pairs={{0,1},{1,0},{2,3},{3,2},{4,5},{5,4},{6,7},{7,6},{8,9},{9,8},{10,11... | collective-permute-start | bytes 356360 | tf_op jit(solution)/shard_map/ppermute | solution.py:297
  36.9 0.0 collective-permute-done.7.refs_4_
  36.9 1.3 %collective-permute-start.12 = (bf16[16,3712]{1,0:T(8,128)(2,1)S(1)}, bf16[16,3712]{1,0:T(8,128)(2,1)S(1)}, u32[]{:S(2)}, u32[]{:S(2)}) collective-permute-start(bf16[16,3712]{1,0:T(8,128)(2,1)S(1)} %collective-permute-done.11.refs_6_), channel_id=1, source_target_pairs={{0,1},{1,0},{2,3},{3,2},{4,5},{5,4},{6,7},{7,6},{8,9},{9,8},{10,11... | collective-permute-start | bytes 356360 | tf_op jit(solution)/shard_map/ppermute | solution.py:297
  38.2 0.0 collective-permute-done.4.refs_1_
  38.2 0.8 %collective-permute-start.14 = (bf16[16,3712]{1,0:T(8,128)(2,1)S(1)}, bf16[16,3712]{1,0:T(8,128)(2,1)S(1)}, u32[]{:S(2)}, u32[]{:S(2)}) collective-permute-start(bf16[16,3712]{1,0:T(8,128)(2,1)S(1)} %collective-permute-done.13.refs_7_), channel_id=1, source_target_pairs={{0,1},{1,0},{2,3},{3,2},{4,5},{5,4},{6,7},{7,6},{8,9},{9,8},{10,11... | collective-permute-start | bytes 356360 | tf_op jit(solution)/shard_map/ppermute | solution.py:297
  39.0 0.0 collective-permute-done.5.refs_2_
  39.0 1.3 %collective-permute-start.8 = (bf16[16,3712]{1,0:T(8,128)(2,1)S(1)}, bf16[16,3712]{1,0:T(8,128)(2,1)S(1)}, u32[]{:S(2)}, u32[]{:S(2)}) collective-permute-start(bf16[16,3712]{1,0:T(8,128)(2,1)S(1)} %collective-permute-done.7.refs_4_), channel_id=1, source_target_pairs={{0,1},{1,0},{2,3},{3,2},{4,5},{5,4},{6,7},{7,6},{8,9},{9,8},{10,11... | collective-permute-start | bytes 356360 | tf_op jit(solution)/shard_map/ppermute | solution.py:297
  40.2 0.0 collective-permute-done.6.refs_3_
  40.2 1.7 %project_first.1 = (f32[2,128,512]{2,1,0:T(8,128)S(1)}, f32[128,128]{1,0:T(8,128)S(1)}) custom-call(s32[2]{0:T(128)S(1)} %pad_add_fusion.place, bf16[2,7168,512]{2,1,0:T(8,128)(2,1)S(1)} %mask_matrices.1.mat_ref, bf16[64,3712]{1,0:T(8,128)(2,1)S(1)} %get-tuple-element.20.own_ref.refs_0_, bf16[32,3712]{1,0:T(8,128)(2,1)S(1)} %collective-permute-done.4.refs_1_, ...), custom_call_target="tpu_custom_call" | custom-call | flops 939524096 | bytes 7340032 | tf_op jit(solution)/shard_map/project_first/pallas_call | solution.py:271
  41.9 0.0 collective-permute-done.10.refs_5_
  42.0 2.1 %collective-permute-done.12.refs_6_ = bf16[16,3712]{1,0:T(8,128)(2,1)S(1)} collective-permute-done((bf16[16,3712]{1,0:T(8,128)(2,1)S(1)}, bf16[16,3712]{1,0:T(8,128)(2,1)S(1)}, u32[]{:S(2)}, u32[]{:S(2)}) %collective-permute-start.12) | collective-permute-done | bytes 118816 | tf_op jit(solution)/shard_map/ppermute | solution.py:297
  44.1 1.4 %collective-permute-done.14.refs_7_ = bf16[16,3712]{1,0:T(8,128)(2,1)S(1)} collective-permute-done((bf16[16,3712]{1,0:T(8,128)(2,1)S(1)}, bf16[16,3712]{1,0:T(8,128)(2,1)S(1)}, u32[]{:S(2)}, u32[]{:S(2)}) %collective-permute-start.14) | collective-permute-done | bytes 118816 | tf_op jit(solution)/shard_map/ppermute | solution.py:297
  45.4 1.3 %collective-permute-done.8.refs_4_ = bf16[16,3712]{1,0:T(8,128)(2,1)S(1)} collective-permute-done((bf16[16,3712]{1,0:T(8,128)(2,1)S(1)}, bf16[16,3712]{1,0:T(8,128)(2,1)S(1)}, u32[]{:S(2)}, u32[]{:S(2)}) %collective-permute-start.8) | collective-permute-done | bytes 118816 | tf_op jit(solution)/shard_map/ppermute | solution.py:297
  46.7 2.4 %project_last.1 = bf16[1,128,512]{2,1,0:T(8,128)(2,1)} custom-call(s32[2]{0:T(128)S(1)} %pad_add_fusion.place, bf16[2,7168,512]{2,1,0:T(8,128)(2,1)S(1)} %mask_matrices.1.mat_ref, bf16[64,3712]{1,0:T(8,128)(2,1)S(1)} %collective-permute-done.3.other_ref.refs_0_, bf16[32,3712]{1,0:T(8,128)(2,1)S(1)} %collective-permute-done.4.refs_1_, ...), custom_call_target="tpu_custom_call" | custom-call | flops 939524096 | bytes 7340032 | tf_op jit(solution)/shard_map/project_last/pallas_call | solution.py:271
  (1 shorter events, 0.0 us)
Async XLA Ops:
  0.0 3.2 %collective-permute-start.2 = (bf16[128,3584]{1,0:T(8,128)(2,1)}, bf16[128,3584]{1,0:T(8,128)(2,1)S(1)}, u32[]{:S(2)}, u32[]{:S(2)}) collective-permute-start(bf16[128,3584]{1,0:T(8,128)(2,1)} %tok_hbm.1), channel_id=1, source_target_pairs={{0,2},{2,0},{4,6},{6,4},{8,10},{10,8},{12,14},{14,12},{16,18},{18,... | collective-permute-start | bytes 2752520 | tf_op jit(solution)/shard_map/ppermute | solution.py:294
  0.5 2.8 %collective-permute-start = (s32[8,128]{1,0:T(8,128)}, s32[8,128]{1,0:T(8,128)S(1)}, u32[]{:S(2)}, u32[]{:S(2)}) collective-permute-start(s32[8,128]{1,0:T(8,128)} %bitcast.10), channel_id=1, source_target_pairs={{0,2},{2,0},{4,6},{6,4},{8,10},{10,8},{12,14},{14,12},{16,18},{18,... | collective-permute-start | bytes 12296 | tf_op jit(solution)/shard_map/ppermute | solution.py:294
  0.5 2.7 %collective-permute-start.1 = (f32[8,128]{1,0:T(8,128)}, f32[8,128]{1,0:T(8,128)S(1)}, u32[]{:S(2)}, u32[]{:S(2)}) collective-permute-start(f32[8,128]{1,0:T(8,128)} %bitcast.12), channel_id=1, source_target_pairs={{0,2},{2,0},{4,6},{6,4},{8,10},{10,8},{12,14},{14,12},{16,18},{18,... | collective-permute-start | bytes 12296 | tf_op jit(solution)/shard_map/ppermute | solution.py:294
  4.3 14.1 %collective-permute-start.3 = (bf16[64,3712]{1,0:T(8,128)(2,1)S(1)}, bf16[64,3712]{1,0:T(8,128)(2,1)S(1)}, u32[]{:S(2)}, u32[]{:S(2)}) collective-permute-start(bf16[64,3712]{1,0:T(8,128)(2,1)S(1)} %get-tuple-element.20.own_ref.refs_0_), channel_id=1, source_target_pairs={{0,1},{1,0},{2,3},{3,2},{4,5},{5,4},{6,7},{7,6},{8,9},{9,8},{10,11... | collective-permute-start | bytes 1425416 | tf_op jit(solution)/shard_map/ppermute | solution.py:297
  6.9 15.2 %collective-permute-start.11 = (bf16[16,3712]{1,0:T(8,128)(2,1)S(1)}, bf16[16,3712]{1,0:T(8,128)(2,1)S(1)}, u32[]{:S(2)}, u32[]{:S(2)}) collective-permute-start(bf16[16,3712]{1,0:T(8,128)(2,1)S(1)} %get-tuple-element.29), channel_id=1, source_target_pairs={{0,24},{2,26},{4,28},{6,30},{8,16},{10,18},{12,20},{14,22},{16,8},... | collective-permute-start | bytes 356360 | tf_op jit(solution)/shard_map/ppermute | solution.py:294
  10.5 15.3 %collective-permute-start.13 = (bf16[16,3712]{1,0:T(8,128)(2,1)S(1)}, bf16[16,3712]{1,0:T(8,128)(2,1)S(1)}, u32[]{:S(2)}, u32[]{:S(2)}) collective-permute-start(bf16[16,3712]{1,0:T(8,128)(2,1)S(1)} %get-tuple-element.30), channel_id=1, source_target_pairs={{0,28},{2,30},{4,24},{6,26},{8,20},{10,22},{12,16},{14,18},{16,12}... | collective-permute-start | bytes 356360 | tf_op jit(solution)/shard_map/ppermute | solution.py:294
  11.7 0.7 %copy-start = (s32[1,2,112,8]{2,3,1,0:T(8,128)S(1)}, s32[1,2,112,8]{2,3,1,0:T(8,128)}, u32[]{:S(2)}) copy-start(s32[1,2,112,8]{2,3,1,0:T(8,128)} %param.9) | copy-start | bytes 21508
  18.5 19.7 %collective-permute-start.4 = (bf16[32,3712]{1,0:T(8,128)(2,1)S(1)}, bf16[32,3712]{1,0:T(8,128)(2,1)S(1)}, u32[]{:S(2)}, u32[]{:S(2)}) collective-permute-start(bf16[32,3712]{1,0:T(8,128)(2,1)S(1)} %get-tuple-element.24), channel_id=1, source_target_pairs={{0,4},{2,6},{4,0},{6,2},{8,12},{10,14},{12,8},{14,10},{16,20},{18,... | collective-permute-start | bytes 712712 | tf_op jit(solution)/shard_map/ppermute | solution.py:294
  20.3 18.7 %collective-permute-start.5 = (bf16[32,3712]{1,0:T(8,128)(2,1)S(1)}, bf16[32,3712]{1,0:T(8,128)(2,1)S(1)}, u32[]{:S(2)}, u32[]{:S(2)}) collective-permute-start(bf16[32,3712]{1,0:T(8,128)(2,1)S(1)} %get-tuple-element.25), channel_id=1, source_target_pairs={{0,8},{2,10},{4,12},{6,14},{8,0},{10,2},{12,4},{14,6},{16,24},{18,... | collective-permute-start | bytes 712712 | tf_op jit(solution)/shard_map/ppermute | solution.py:294
  21.9 18.4 %collective-permute-start.6 = (bf16[32,3712]{1,0:T(8,128)(2,1)S(1)}, bf16[32,3712]{1,0:T(8,128)(2,1)S(1)}, u32[]{:S(2)}, u32[]{:S(2)}) collective-permute-start(bf16[32,3712]{1,0:T(8,128)(2,1)S(1)} %get-tuple-element.26), channel_id=1, source_target_pairs={{0,12},{2,14},{4,8},{6,10},{8,4},{10,6},{12,0},{14,2},{16,28},{18,... | collective-permute-start | bytes 712712 | tf_op jit(solution)/shard_map/ppermute | solution.py:294
  22.1 13.4 %collective-permute-start.9 = (bf16[16,3712]{1,0:T(8,128)(2,1)S(1)}, bf16[16,3712]{1,0:T(8,128)(2,1)S(1)}, u32[]{:S(2)}, u32[]{:S(2)}) collective-permute-start(bf16[16,3712]{1,0:T(8,128)(2,1)S(1)} %get-tuple-element.28), channel_id=1, source_target_pairs={{0,20},{2,22},{4,16},{6,18},{8,28},{10,30},{12,24},{14,26},{16,4},... | collective-permute-start | bytes 356360 | tf_op jit(solution)/shard_map/ppermute | solution.py:294
  25.8 11.1 %collective-permute-start.7 = (bf16[16,3712]{1,0:T(8,128)(2,1)S(1)}, bf16[16,3712]{1,0:T(8,128)(2,1)S(1)}, u32[]{:S(2)}, u32[]{:S(2)}) collective-permute-start(bf16[16,3712]{1,0:T(8,128)(2,1)S(1)} %get-tuple-element.27), channel_id=1, source_target_pairs={{0,16},{2,18},{4,20},{6,22},{8,24},{10,26},{12,28},{14,30},{16,0},... | collective-permute-start | bytes 356360 | tf_op jit(solution)/shard_map/ppermute | solution.py:294
  35.4 6.5 %collective-permute-start.10 = (bf16[16,3712]{1,0:T(8,128)(2,1)S(1)}, bf16[16,3712]{1,0:T(8,128)(2,1)S(1)}, u32[]{:S(2)}, u32[]{:S(2)}) collective-permute-start(bf16[16,3712]{1,0:T(8,128)(2,1)S(1)} %collective-permute-done.9.refs_5_), channel_id=1, source_target_pairs={{0,1},{1,0},{2,3},{3,2},{4,5},{5,4},{6,7},{7,6},{8,9},{9,8},{10,11... | collective-permute-start | bytes 356360 | tf_op jit(solution)/shard_map/ppermute | solution.py:297
  36.9 7.2 %collective-permute-start.12 = (bf16[16,3712]{1,0:T(8,128)(2,1)S(1)}, bf16[16,3712]{1,0:T(8,128)(2,1)S(1)}, u32[]{:S(2)}, u32[]{:S(2)}) collective-permute-start(bf16[16,3712]{1,0:T(8,128)(2,1)S(1)} %collective-permute-done.11.refs_6_), channel_id=1, source_target_pairs={{0,1},{1,0},{2,3},{3,2},{4,5},{5,4},{6,7},{7,6},{8,9},{9,8},{10,11... | collective-permute-start | bytes 356360 | tf_op jit(solution)/shard_map/ppermute | solution.py:297
  38.2 7.2 %collective-permute-start.14 = (bf16[16,3712]{1,0:T(8,128)(2,1)S(1)}, bf16[16,3712]{1,0:T(8,128)(2,1)S(1)}, u32[]{:S(2)}, u32[]{:S(2)}) collective-permute-start(bf16[16,3712]{1,0:T(8,128)(2,1)S(1)} %collective-permute-done.13.refs_7_), channel_id=1, source_target_pairs={{0,1},{1,0},{2,3},{3,2},{4,5},{5,4},{6,7},{7,6},{8,9},{9,8},{10,11... | collective-permute-start | bytes 356360 | tf_op jit(solution)/shard_map/ppermute | solution.py:297
  39.0 7.8 %collective-permute-start.8 = (bf16[16,3712]{1,0:T(8,128)(2,1)S(1)}, bf16[16,3712]{1,0:T(8,128)(2,1)S(1)}, u32[]{:S(2)}, u32[]{:S(2)}) collective-permute-start(bf16[16,3712]{1,0:T(8,128)(2,1)S(1)} %collective-permute-done.7.refs_4_), channel_id=1, source_target_pairs={{0,1},{1,0},{2,3},{3,2},{4,5},{5,4},{6,7},{7,6},{8,9},{9,8},{10,11... | collective-permute-start | bytes 356360 | tf_op jit(solution)/shard_map/ppermute | solution.py:297

commit v2 on v1

--- a/solution.py
+++ b/solution.py
@@ -11,6 +11,7 @@
 CAP = 8
 LANES = 128
 PAIR = 2 * CAP
+PIECES = 8
 
 
 def expand_mask(keep_mask, block_size):
@@ -110,22 +111,21 @@
     out_ref[:, width:] = jnp.broadcast_to(weights, (weights.shape[0], LANES)).astype(out_ref.dtype)
 
 
-def pair_kernel(groups, near, place, ids_ref, wgt_ref, tok_ref, own_ref, near_ref, *far_refs):
+def pair_kernel(groups, place, ids_ref, wgt_ref, tok_ref, own_ref, *out_refs):
     picks, weights = chosen_rows(groups, place, 1, ids_ref[...], wgt_ref[...])
     width = tok_ref.shape[1]
 
     def put(span, got):
-        got = (got + own_ref[:, span].astype(jnp.float32)).astype(near_ref.dtype)
-        near_ref[:, span] = got[: PAIR * near]
-        for k, far_ref in enumerate(far_refs):
-            far_ref[:, span] = got[PAIR * (near + k) : PAIR * (near + k + 1)]
+        got = (got + own_ref[:, span].astype(jnp.float32)).astype(own_ref.dtype)
+        for k, out_ref in enumerate(out_refs):
+            out_ref[:, span] = got[PAIR * k : PAIR * (k + 1)]
 
     for span in spans(width):
         put(span, jnp.dot(picks, tok_ref[:, span], preferred_element_type=jnp.float32))
     put(slice(width, width + LANES), jnp.broadcast_to(weights, (weights.shape[0], LANES)))
 
 
-def dispatch(place, ids, wgt, tok, partner, groups, near):
+def dispatch(place, ids, wgt, tok, partner, groups):
     count, width = tok.shape
     smem = pl.BlockSpec(memory_space=pltpu.SMEM)
     vmem = pl.BlockSpec(memory_space=pltpu.VMEM)
@@ -143,10 +143,9 @@
         cost_estimate=cost,
         name="own_rows",
     )(place, *(pltpu.with_memory_space_constraint(a, pltpu.HBM) for a in (ids, wgt, tok)))
-    shapes = [jax.ShapeDtypeStruct((PAIR * near, width + LANES), tok.dtype)]
-    shapes += [jax.ShapeDtypeStruct((PAIR, width + LANES), tok.dtype)] * (groups - near)
+    shapes = [jax.ShapeDtypeStruct((PAIR, width + LANES), tok.dtype)] * groups
     return pl.pallas_call(
-        functools.partial(pair_kernel, groups, near),
+        functools.partial(pair_kernel, groups),
         out_shape=shapes,
         in_specs=[smem] + [vmem] * 4,
         out_specs=[vmem] * len(shapes),
@@ -156,96 +155,88 @@
     )(place, *partner, own)
 
 
-def mask_kernel(keep_ref, mat_hbm, out_ref, mask_ref, sems):
-    parts = sems.shape[1]
-    units, depth = out_ref.shape[2], out_ref.shape[1] // parts
+def mask_kernel(m, keep_ref, mat_hbm, out_ref, mask_ref, sems):
+    parts = sems.shape[0]
+    units, depth = out_ref.shape[1], out_ref.shape[0] // parts
     copies = [
-        [
-            pltpu.make_async_copy(
-                mat_hbm.at[m, pl.ds(p * depth, depth)], out_ref.at[m, pl.ds(p * depth, depth)], sems.at[m, p]
-            )
-            for p in range(parts)
-        ]
-        for m in range(2)
+        pltpu.make_async_copy(
+            mat_hbm.at[m, pl.ds(p * depth, depth)], out_ref.at[pl.ds(p * depth, depth)], sems.at[p]
+        )
+        for p in range(parts)
     ]
-    for p in range(parts):
-        for m in range(2):
-            copies[m][p].start()
+    for copy in copies:
+        copy.start()
     cols = keep_ref.shape[1]
     lane = lax.broadcasted_iota(jnp.int32, (cols, units), 1) // BLOCK
     row = lax.broadcasted_iota(jnp.int32, (cols, units), 0)
-    widen = (lane == row).astype(jnp.bfloat16)
-    for m in range(2):
-        mask_ref[m] = lax.dot_general(
-            keep_ref[m].astype(jnp.float32).astype(jnp.bfloat16),
-            widen,
-            (((0,), (0,)), ((), ())),
-            preferred_element_type=jnp.float32,
-        )
-    for p in range(parts):
-        for m in range(2):
-            copies[m][p].wait()
-
-            @pl.loop(0, depth // BLOCK)
-            def _(r):
-                at = p * (depth // BLOCK) + r
-                keep = mask_ref[m, pl.ds(at, 1), :].astype(out_ref.dtype)
-                span = pl.ds(pl.multiple_of(at * BLOCK, BLOCK), BLOCK)
-                out_ref[m, span, :] = out_ref[m, span, :] * keep
-
-
-def mask_matrices(keep, matrices):
+    mask_ref[...] = lax.dot_general(
+        keep_ref[m].astype(jnp.float32).astype(jnp.bfloat16),
+        (lane == row).astype(jnp.bfloat16),
+        (((0,), (0,)), ((), ())),
+        preferred_element_type=jnp.float32,
+    )
+    for p, copy in enumerate(copies):
+        copy.wait()
+
+        @pl.loop(0, depth // BLOCK)
+        def _(r):
+            at = p * (depth // BLOCK) + r
+            keep = mask_ref[pl.ds(at, 1), :].astype(out_ref.dtype)
+            span = pl.ds(pl.multiple_of(at * BLOCK, BLOCK), BLOCK)
+            out_ref[span, :] = out_ref[span, :] * keep
+
+
+def mask_matrix(keep, matrices, m):
     rows, units = matrices.shape[1:]
     parts = next(p for p in (14, 16, 8, 7, 4, 2, 1) if rows % (p * BLOCK) == 0)
     vmem = pl.BlockSpec(memory_space=pltpu.VMEM)
     return pl.pallas_call(
-        mask_kernel,
-        out_shape=jax.ShapeDtypeStruct(matrices.shape, matrices.dtype),
+        functools.partial(mask_kernel, m),
+        out_shape=jax.ShapeDtypeStruct(matrices.shape[1:], matrices.dtype),
         in_specs=[vmem, pl.BlockSpec(memory_space=pl.ANY)],
         out_specs=vmem,
-        scratch_shapes=[pltpu.VMEM((2, rows // BLOCK, units), jnp.float32), pltpu.SemaphoreType.DMA((2, parts))],
-        compiler_params=pltpu.CompilerParams(vmem_limit_bytes=20 << 20),
-        cost_estimate=pl.CostEstimate(flops=2 * rows * units, bytes_accessed=4 * rows * units, transcendentals=0),
-        name="mask_matrices",
+        scratch_shapes=[pltpu.VMEM((rows // BLOCK, units), jnp.float32), pltpu.SemaphoreType.DMA((parts,))],
+        compiler_params=pltpu.CompilerParams(vmem_limit_bytes=10 << 20),
+        cost_estimate=pl.CostEstimate(flops=8 * rows * units, bytes_accessed=8 * rows * units, transcendentals=0),
+        name="mask_matrix",
     )(keep, pltpu.with_memory_space_constraint(matrices, pltpu.HBM))
 
 
-def join_kernel(near, own_ref, other_ref, *out_refs):
-    for k, out_ref in enumerate(out_refs):
-        span = slice(PAIR * (k + 1), PAIR * (k + 2))
-        out_ref[:PAIR] = own_ref[span]
-        out_ref[PAIR:] = other_ref[span]
-
-
-def join(own, other, near):
+def join_kernel(*refs):
+    *piece_refs, out_ref = refs
+    for k, piece_ref in enumerate(piece_refs):
+        out_ref[PAIR * k : PAIR * (k + 1)] = piece_ref[...]
+
+
+def join(*pieces):
     vmem = pl.BlockSpec(memory_space=pltpu.VMEM)
     return pl.pallas_call(
-        functools.partial(join_kernel, near),
-        out_shape=[jax.ShapeDtypeStruct((2 * PAIR, own.shape[1]), own.dtype)] * (near - 1),
-        in_specs=[vmem] * 2,
-        out_specs=[vmem] * (near - 1),
+        join_kernel,
+        out_shape=jax.ShapeDtypeStruct((PAIR * len(pieces), pieces[0].shape[1]), pieces[0].dtype),
+        in_specs=[vmem] * len(pieces),
+        out_specs=vmem,
         compiler_params=pltpu.CompilerParams(vmem_limit_bytes=4 << 20),
         name="join",
-    )(own, other)
-
-
-def project_kernel(groups, near, last, place, mat_ref, *refs):
-    pieces, refs = refs[:groups], refs[groups:]
+    )(*pieces)
+
+
+def project_kernel(where, last, place, gate_ref, up_ref, *refs):
+    count = 1 + max(i for i, _ in where)
+    pieces, refs = refs[:count], refs[count:]
     if last:
         total_ref, scale_ref, out_ref, x_ref = refs
     else:
         total_ref, scale_ref, x_ref = refs
     chip = place[0] // 2
     width = x_ref.shape[1]
-    for k in range(groups):
+    for k, (i, row) in enumerate(where):
         at = pl.multiple_of(PAIR * (chip ^ k), PAIR)
-        half = slice(PAIR, None) if last and 0 < k < near else slice(0, PAIR)
-        x_ref[pl.ds(at, PAIR), :] = pieces[k][half, :width]
+        x_ref[pl.ds(at, PAIR), :] = pieces[i][row : row + PAIR, :width]
         if not last:
-            scale_ref[pl.ds(at, PAIR), :] = pieces[k][:PAIR, width:].astype(jnp.float32)
+            scale_ref[pl.ds(at, PAIR), :] = pieces[i][row : row + PAIR, width:].astype(jnp.float32)
     share = 1 - place[1] if last else place[1]
     span = pl.ds(pl.multiple_of(share * width, BLOCK), width)
-    totals = [jnp.dot(x_ref[...], mat_ref[m, span, :], preferred_element_type=jnp.float32) for m in range(2)]
+    totals = [jnp.dot(x_ref[...], ref[span, :], preferred_element_type=jnp.float32) for ref in (gate_ref, up_ref)]
     if last:
         gate, up = (total_ref[m] + totals[m] for m in range(2))
         out_ref[0] = (scale_ref[:, :1] * (gate / (1.0 + jnp.exp(-gate))) * up).astype(out_ref.dtype)
@@ -254,12 +245,12 @@
             total_ref[m] = totals[m]
 
 
-def project(place, matrices, pieces, groups, near, width, total=None, scale=None):
+def project(place, matrices, pieces, where, width, total=None, scale=None):
     last = total is not None
-    units = matrices.shape[2]
-    slots = PAIR * groups
+    units = matrices[0].shape[1]
+    slots = PAIR * len(where)
     vmem = pl.BlockSpec(memory_space=pltpu.VMEM)
-    args = [place, matrices, *pieces]
+    args = [place, *matrices, *pieces]
     if last:
         args += [total, scale]
         out_shape = jax.ShapeDtypeStruct((1, slots, units), jnp.bfloat16)
@@ -269,7 +260,7 @@
             jax.ShapeDtypeStruct((slots, LANES), jnp.float32),
         ]
     return pl.pallas_call(
-        functools.partial(project_kernel, groups, near, last),
+        functools.partial(project_kernel, where, last),
         out_shape=out_shape,
         in_specs=[pl.BlockSpec(memory_space=pltpu.SMEM)] + [vmem] * (len(args) - 1),
         out_specs=vmem if last else [vmem, vmem],
@@ -296,30 +287,36 @@
     def cross(a):
         return lax.ppermute(a, "tensor", [(0, 1), (1, 0)])
 
+    def after(a, *done):
+        return lax.optimization_barrier((a, done))[0]
+
     ids, wgt = route_ids.T, route_weight.T
     partner = [move(a, 1) for a in (ids, wgt, tokens)]
-    own, *far = dispatch(place, ids, wgt, tokens, partner, groups, near)
+    piece = list(dispatch(place, ids, wgt, tokens, partner, groups))
     keep = jnp.swapaxes(block_keep[0], 1, 2)
-    keep, own = lax.optimization_barrier((keep, own))
-    masked = mask_matrices(keep, gate_up[0])
-    far_order = sorted(range(groups - near), key=lambda k: (k % 2, -k))
-    far_in = [None] * (groups - near)
-    for k in far_order:
-        far_in[k] = move(far[k], 2 * (near + k))
-    other, masked = lax.optimization_barrier((cross(own), masked))
-    both = join(own, other, near)
-    near_in = [move(b, 2 * (k + 1)) for k, b in enumerate(both)]
-    far_other = [None] * (groups - near)
-    for k in far_order:
-        far_other[k] = cross(far_in[k])
-
-    total, scale = project(place, masked, [own, *near_in, *far_in], groups, near, width)
-    return project(place, masked, [other, *near_in, *far_other], groups, near, width, total, scale)
+    got, other = [piece[0]] + [None] * (groups - 1), [None] * groups
+    got[4] = move(piece[4], 8)
+    got[6] = move(piece[6], 12)
+    got[3] = move(piece[3], 6)
+    got[2] = move(piece[2], 4)
+    got[1] = move(piece[1], 2)
+    up = mask_matrix(after(keep, piece[0]), gate_up[0], 1)
+    got[7] = move(piece[7], 14)
+    got[5] = move(piece[5], 10)
+    gate = mask_matrix(after(keep, piece[0]), gate_up[0], 0)
+    block1 = cross(got[3])
+    block2 = cross(join(got[4], after(got[7], up)))
+    block0 = cross(join(got[0], got[1], got[2]))
+    block4 = cross(after(got[6], block1))
+    block3 = cross(after(got[5], up, got[7]))
+    masked = (gate, up)
+    total, scale = project(place, masked, got, [(k, 0) for k in range(groups)], width)
+    where = [(0, 0), (0, 16), (0, 32), (1, 0), (2, 0), (3, 0), (4, 0), (2, 16)]
+    return project(place, masked, [block0, block1, block2, block3, block4], where, width, total, scale)
 
 
 def solution(mesh):
-    shares, experts = mesh.shape["tensor"], mesh.shape["expert"]
-    paired = shares == 2 and 8 <= experts <= 16 and experts & (experts - 1) == 0
+    paired = mesh.shape["tensor"] == 2 and mesh.shape["expert"] == 2 * PIECES
     return jax.shard_map(
         paired_form if paired else gathered_form,
         mesh=mesh,

time: 49.9 us -> 40.8 us (0.82); the launches traced: 49.1 us -> 40.6 us
  waiting for transfers between devices: 14.6 us -> 3.05 us
  starting transfers between devices: 20.7 us -> 22.7 us
  Pallas kernels: 12.9 us -> 13.9 us
    ppermute x10, waiting for transfers between devices: 9.3 us -> 1.82 us  [move(): return lax.ppermute(a, 'expert', [(s, s ^ shift) for s in range(n)])]
    ppermute x5, waiting for transfers between devices: 5.33 us -> 1.23 us  [cross(): return lax.ppermute(a, 'tensor', [(0, 1), (1, 0)])]
    ppermute x10, starting transfers between devices: 13.3 us -> 15.7 us  [move(): return lax.ppermute(a, 'expert', [(s, s ^ shift) for s in range(n)])]
    pallas_call x5 -> x7, Pallas kernels: 10.7 us -> 11.8 us  [the longest x2 6.58 us: mask_matrix(): pl.pallas_call(functools.partial(mask_kernel, m), out_shape=jax.ShapeDtyp...]
  transfers between devices with their start and end apart: 15 -> 15, of which waited for: 5 -> 3; matrix products, arithmetic and copies ran while one was open for 0% -> 0% of each run, Pallas kernels for 19% -> 26%
where the time goes in v2:
time: 40.8 us; the launch traced here: 40.6 us
  starting transfers between devices  22.7 us (56%)
  Pallas kernels  13.9 us (34%)
  waiting for transfers between devices  3.05 us (7%)
  local copies, waits for them, and re-layouts  0.7 us (2%)
    ppermute x10, starting transfers between devices, move(): return lax.ppermute(a, 'expert', [(s, s ^ shift) for s in range(n)])  15.7 us
    ppermute x5, starting transfers between devices, cross(): return lax.ppermute(a, 'tensor', [(0, 1), (1, 0)])  7.06 us
    pallas_call x2, Pallas kernels, mask_matrix(): pl.pallas_call(functools.partial(mask_kernel, m), out_shape=jax.ShapeDtyp...  6.58 us
    pallas_call x2, Pallas kernels, project(): pl.pallas_call(functools.partial(project_kernel, where, last), out_shape=...  4.06 us
    pallas_call x1, Pallas kernels, dispatch(): pl.pallas_call(functools.partial(own_kernel, groups), out_shape=jax.Shape...  2.17 us
    ppermute x10, waiting for transfers between devices, move(): return lax.ppermute(a, 'expert', [(s, s ^ shift) for s in range(n)])  1.82 us
    ppermute x5, waiting for transfers between devices, cross(): return lax.ppermute(a, 'tensor', [(0, 1), (1, 0)])  1.23 us
    pallas_call x1, Pallas kernels, dispatch(): pl.pallas_call(functools.partial(pair_kernel, groups), out_shape=shapes,...  1.08 us
  transfers between devices with their start and end apart: 15, of which 3 were waited for; matrix products, arithmetic and copies ran while one was open for 0% of the time, Pallas kernels for 26%

profile of v2, /device:TPU:0, one launch (start us, length us, event | category | flops | bytes accessed | tf_op | source)
XLA Modules:
  0.0 40.6 jit_solution(13581511164468257202)
XLA Ops:
  0.0 0.5 %collective-permute-start.2 = (bf16[128,3584]{1,0:T(8,128)(2,1)}, bf16[128,3584]{1,0:T(8,128)(2,1)S(1)}, u32[]{:S(2)}, u32[]{:S(2)}) collective-permute-start(bf16[128,3584]{1,0:T(8,128)(2,1)} %tok_hbm.1), channel_id=1, source_target_pairs={{0,2},{2,0},{4,6},{6,4},{8,10},{10,8},{12,14},{14,12},{16,18},{18,... | collective-permute-start | bytes 2752520 | tf_op jit(solution)/shard_map/ppermute | solution.py:285
  0.5 0.1 collective-permute-start
  0.5 0.5 %collective-permute-start.1 = (f32[8,128]{1,0:T(8,128)}, f32[8,128]{1,0:T(8,128)S(1)}, u32[]{:S(2)}, u32[]{:S(2)}) collective-permute-start(f32[8,128]{1,0:T(8,128)} %bitcast.14), channel_id=1, source_target_pairs={{0,2},{2,0},{4,6},{6,4},{8,10},{10,8},{12,14},{14,12},{16,18},{18,... | collective-permute-start | bytes 12296 | tf_op jit(solution)/shard_map/ppermute | solution.py:285
  1.0 0.1 pad_add_fusion.place
  1.0 2.2 %own_rows.1.own_ref = bf16[128,3712]{1,0:T(8,128)(2,1)S(1)} custom-call(s32[2]{0:T(128)S(1)} %pad_add_fusion.place, s32[8,128]{1,0:T(8,128)} %bitcast.13, f32[8,128]{1,0:T(8,128)} %bitcast.15, bf16[128,3584]{1,0:T(8,128)(2,1)} %tok_hbm.1), custom_call_target="tpu_custom_call" | custom-call | flops 117440512 | bytes 917504 | tf_op jit(solution)/shard_map/own_rows/pallas_call | solution.py:136
  3.2 0.0 collective-permute-done.ids_ref
  3.2 0.0 collective-permute-done.1.wgt_ref
  3.2 0.0 collective-permute-done.2.tok_ref
  3.3 1.1 %pair_rows.1 = (bf16[16,3712]{1,0:T(8,128)(2,1)S(1)}, bf16[16,3712]{1,0:T(8,128)(2,1)S(1)}, bf16[16,3712]{1,0:T(8,128)(2,1)S(1)}, bf16[16,3712]{1,0:T(8,128)(2,1...) custom-call(s32[2]{0:T(128)S(1)} %pad_add_fusion.place, ...), custom_call_target="tpu_custom_call" | custom-call | flops 117440512 | bytes 917504 | tf_op jit(solution)/shard_map/pair_rows/pallas_call | solution.py:147
  4.3 2.5 %collective-permute-start.3 = (bf16[16,3712]{1,0:T(8,128)(2,1)S(1)}, bf16[16,3712]{1,0:T(8,128)(2,1)S(1)}, u32[]{:S(2)}, u32[]{:S(2)}) collective-permute-start(bf16[16,3712]{1,0:T(8,128)(2,1)S(1)} %get-tuple-element.21), channel_id=1, source_target_pairs={{0,4},{2,6},{4,0},{6,2},{8,12},{10,14},{12,8},{14,10},{16,20},{18,... | collective-permute-start | bytes 356360 | tf_op jit(solution)/shard_map/ppermute | solution.py:285
  6.9 1.6 %collective-permute-start.4 = (bf16[16,3712]{1,0:T(8,128)(2,1)S(1)}, bf16[16,3712]{1,0:T(8,128)(2,1)S(1)}, u32[]{:S(2)}, u32[]{:S(2)}) collective-permute-start(bf16[16,3712]{1,0:T(8,128)(2,1)S(1)} %get-tuple-element.22), channel_id=1, source_target_pairs={{0,8},{2,10},{4,12},{6,14},{8,0},{10,2},{12,4},{14,6},{16,24},{18,... | collective-permute-start | bytes 356360 | tf_op jit(solution)/shard_map/ppermute | solution.py:285
  8.5 2.4 %collective-permute-start.9 = (bf16[16,3712]{1,0:T(8,128)(2,1)S(1)}, bf16[16,3712]{1,0:T(8,128)(2,1)S(1)}, u32[]{:S(2)}, u32[]{:S(2)}) collective-permute-start(bf16[16,3712]{1,0:T(8,128)(2,1)S(1)} %get-tuple-element.25), channel_id=1, source_target_pairs={{0,28},{2,30},{4,24},{6,26},{8,20},{10,22},{12,16},{14,18},{16,12}... | collective-permute-start | bytes 356360 | tf_op jit(solution)/shard_map/ppermute | solution.py:285
  10.9 1.6 %collective-permute-start.6 = (bf16[16,3712]{1,0:T(8,128)(2,1)S(1)}, bf16[16,3712]{1,0:T(8,128)(2,1)S(1)}, u32[]{:S(2)}, u32[]{:S(2)}) collective-permute-start(bf16[16,3712]{1,0:T(8,128)(2,1)S(1)} %get-tuple-element.23), channel_id=1, source_target_pairs={{0,12},{2,14},{4,8},{6,10},{8,4},{10,6},{12,0},{14,2},{16,28},{18,... | collective-permute-start | bytes 356360 | tf_op jit(solution)/shard_map/ppermute | solution.py:285
  12.5 1.2 %collective-permute-start.8 = (bf16[16,3712]{1,0:T(8,128)(2,1)S(1)}, bf16[16,3712]{1,0:T(8,128)(2,1)S(1)}, u32[]{:S(2)}, u32[]{:S(2)}) collective-permute-start(bf16[16,3712]{1,0:T(8,128)(2,1)S(1)} %get-tuple-element.24), channel_id=1, source_target_pairs={{0,16},{2,18},{4,20},{6,22},{8,24},{10,26},{12,28},{14,30},{16,0},... | collective-permute-start | bytes 356360 | tf_op jit(solution)/shard_map/ppermute | solution.py:285
  13.7 0.0 collective-permute-done.3.refs_1_
  13.7 0.0 collective-permute-done.4.refs_2_
  13.8 1.6 %collective-permute-start.5 = (bf16[48,3712]{1,0:T(8,128)(2,1)S(1)}, bf16[48,3712]{1,0:T(8,128)(2,1)S(1)}, u32[]{:S(2)}, u32[]{:S(2)}) collective-permute-start(bf16[48,3712]{1,0:T(8,128)(2,1)S(1)} %join.2), channel_id=1, source_target_pairs={{0,1},{1,0},{2,3},{3,2},{4,5},{5,4},{6,7},{7,6},{8,9},{9,8},{10,11... | collective-permute-start | bytes 1069064 | tf_op jit(solution)/shard_map/ppermute | solution.py:288
  15.4 1.7 %collective-permute-start.11 = (bf16[16,3712]{1,0:T(8,128)(2,1)S(1)}, bf16[16,3712]{1,0:T(8,128)(2,1)S(1)}, u32[]{:S(2)}, u32[]{:S(2)}) collective-permute-start(bf16[16,3712]{1,0:T(8,128)(2,1)S(1)} %get-tuple-element.27), channel_id=1, source_target_pairs={{0,20},{2,22},{4,16},{6,18},{8,28},{10,30},{12,24},{14,26},{16,4},... | collective-permute-start | bytes 356360 | tf_op jit(solution)/shard_map/ppermute | solution.py:285
  17.0 0.0 copy-start
  17.0 0.7 %copy-done = s32[1,2,112,8]{2,3,1,0:T(8,128)S(1)} copy-done((s32[1,2,112,8]{2,3,1,0:T(8,128)S(1)}, s32[1,2,112,8]{2,3,1,0:T(8,128)}, u32[]{:S(2)}) %copy-start) | copy-done | bytes 7192
  17.7 3.3 %mask_matrix.3.up_ref = bf16[7168,512]{1,0:T(8,128)(2,1)S(1)} custom-call(s32[2,8,112]{2,1,0:T(8,128)S(1)} %bitcast.8, bf16[2,7168,512]{2,1,0:T(8,128)(2,1)} %bitcast.10), custom_call_target="tpu_custom_call" | custom-call | flops 29360128 | bytes 29360128 | tf_op jit(solution)/shard_map/mask_matrix/pallas_call | solution.py:193
  21.0 0.0 collective-permute-done.9.refs_1_.refs_7_
  21.0 3.6 %collective-permute-start.13 = (bf16[16,3712]{1,0:T(8,128)(2,1)S(1)}, bf16[16,3712]{1,0:T(8,128)(2,1)S(1)}, u32[]{:S(2)}, u32[]{:S(2)}) collective-permute-start(bf16[16,3712]{1,0:T(8,128)(2,1)S(1)} %get-tuple-element.29), channel_id=1, source_target_pairs={{0,24},{2,26},{4,28},{6,30},{8,16},{10,18},{12,20},{14,22},{16,8},... | collective-permute-start | bytes 356360 | tf_op jit(solution)/shard_map/ppermute | solution.py:285
  24.7 0.0 collective-permute-done.6.refs_3_
  24.7 0.6 %collective-permute-start.7 = (bf16[16,3712]{1,0:T(8,128)(2,1)S(1)}, bf16[16,3712]{1,0:T(8,128)(2,1)S(1)}, u32[]{:S(2)}, u32[]{:S(2)}) collective-permute-start(bf16[16,3712]{1,0:T(8,128)(2,1)S(1)} %collective-permute-done.6.refs_3_), channel_id=1, source_target_pairs={{0,1},{1,0},{2,3},{3,2},{4,5},{5,4},{6,7},{7,6},{8,9},{9,8},{10,11... | collective-permute-start | bytes 356360 | tf_op jit(solution)/shard_map/ppermute | solution.py:288
  25.3 0.9 %collective-permute-done.8.refs_0_.refs_4_ = bf16[16,3712]{1,0:T(8,128)(2,1)S(1)} collective-permute-done((bf16[16,3712]{1,0:T(8,128)(2,1)S(1)}, bf16[16,3712]{1,0:T(8,128)(2,1)S(1)}, u32[]{:S(2)}, u32[]{:S(2)}) %collective-permute-start.8) | collective-permute-done | bytes 118816 | tf_op jit(solution)/shard_map/ppermute | solution.py:285
  26.2 2.9 %collective-permute-start.10 = (bf16[32,3712]{1,0:T(8,128)(2,1)S(1)}, bf16[32,3712]{1,0:T(8,128)(2,1)S(1)}, u32[]{:S(2)}, u32[]{:S(2)}) collective-permute-start(bf16[32,3712]{1,0:T(8,128)(2,1)S(1)} %join.3), channel_id=1, source_target_pairs={{0,1},{1,0},{2,3},{3,2},{4,5},{5,4},{6,7},{7,6},{8,9},{9,8},{10,11... | collective-permute-start | bytes 712712 | tf_op jit(solution)/shard_map/ppermute | solution.py:288
  29.1 0.9 %collective-permute-done.11.refs_5_ = bf16[16,3712]{1,0:T(8,128)(2,1)S(1)} collective-permute-done((bf16[16,3712]{1,0:T(8,128)(2,1)S(1)}, bf16[16,3712]{1,0:T(8,128)(2,1)S(1)}, u32[]{:S(2)}, u32[]{:S(2)}) %collective-permute-start.11) | collective-permute-done | bytes 118816 | tf_op jit(solution)/shard_map/ppermute | solution.py:285
  29.9 1.5 %collective-permute-start.12 = (bf16[16,3712]{1,0:T(8,128)(2,1)S(1)}, bf16[16,3712]{1,0:T(8,128)(2,1)S(1)}, u32[]{:S(2)}, u32[]{:S(2)}) collective-permute-start(bf16[16,3712]{1,0:T(8,128)(2,1)S(1)} %collective-permute-done.11.refs_5_), channel_id=1, source_target_pairs={{0,1},{1,0},{2,3},{3,2},{4,5},{5,4},{6,7},{7,6},{8,9},{9,8},{10,11... | collective-permute-start | bytes 356360 | tf_op jit(solution)/shard_map/ppermute | solution.py:288
  31.4 0.0 collective-permute-done.13.refs_6_
  31.4 0.0 collective-permute-done.7.refs_1_
  31.4 0.6 %collective-permute-start.14 = (bf16[16,3712]{1,0:T(8,128)(2,1)S(1)}, bf16[16,3712]{1,0:T(8,128)(2,1)S(1)}, u32[]{:S(2)}, u32[]{:S(2)}) collective-permute-start(bf16[16,3712]{1,0:T(8,128)(2,1)S(1)} %collective-permute-done.13.refs_6_), channel_id=1, source_target_pairs={{0,1},{1,0},{2,3},{3,2},{4,5},{5,4},{6,7},{7,6},{8,9},{9,8},{10,11... | collective-permute-start | bytes 356360 | tf_op jit(solution)/shard_map/ppermute | solution.py:288
  32.0 3.3 %mask_matrix.2.gate_ref = bf16[7168,512]{1,0:T(8,128)(2,1)S(1)} custom-call(s32[2,8,112]{2,1,0:T(8,128)S(1)} %bitcast.9, bf16[2,7168,512]{2,1,0:T(8,128)(2,1)} %bitcast.11), custom_call_target="tpu_custom_call" | custom-call | flops 29360128 | bytes 29360128 | tf_op jit(solution)/shard_map/mask_matrix/pallas_call | solution.py:193
  35.3 1.7 %project_first.1 = (f32[2,128,512]{2,1,0:T(8,128)S(1)}, f32[128,128]{1,0:T(8,128)S(1)}) custom-call(s32[2]{0:T(128)S(1)} %pad_add_fusion.place, bf16[7168,512]{1,0:T(8,128)(2,1)S(1)} %mask_matrix.2.gate_ref, bf16[7168,512]{1,0:T(8,128)(2,1)S(1)} %mask_matrix.3.up_ref, bf16[16,3712]{1,0:T(8,128)(2,1)S(1)} %get-tuple-element.19.refs_0_, ...), custom_call_target="tpu_custom_call" | custom-call | flops 939524096 | bytes 7340032 | tf_op jit(solution)/shard_map/project_first/pallas_call | solution.py:262
  37.0 0.0 collective-permute-done.12.refs_3_
  37.0 0.0 collective-permute-done.10.refs_2_
  37.0 1.2 %collective-permute-done.14.refs_4_ = bf16[16,3712]{1,0:T(8,128)(2,1)S(1)} collective-permute-done((bf16[16,3712]{1,0:T(8,128)(2,1)S(1)}, bf16[16,3712]{1,0:T(8,128)(2,1)S(1)}, u32[]{:S(2)}, u32[]{:S(2)}) %collective-permute-start.14) | collective-permute-done | bytes 118816 | tf_op jit(solution)/shard_map/ppermute | solution.py:288
  38.2 0.0 collective-permute-done.5.refs_0_
  38.2 2.4 %project_last.1 = bf16[1,128,512]{2,1,0:T(8,128)(2,1)} custom-call(s32[2]{0:T(128)S(1)} %pad_add_fusion.place, bf16[7168,512]{1,0:T(8,128)(2,1)S(1)} %mask_matrix.2.gate_ref, bf16[7168,512]{1,0:T(8,128)(2,1)S(1)} %mask_matrix.3.up_ref, bf16[48,3712]{1,0:T(8,128)(2,1)S(1)} %collective-permute-done.5.refs_0_, ...), custom_call_target="tpu_custom_call" | custom-call | flops 939524096 | bytes 7340032 | tf_op jit(solution)/shard_map/project_last/pallas_call | solution.py:262
  (2 shorter events, 0.0 us)
Async XLA Ops:
  0.0 3.2 %collective-permute-start.2 = (bf16[128,3584]{1,0:T(8,128)(2,1)}, bf16[128,3584]{1,0:T(8,128)(2,1)S(1)}, u32[]{:S(2)}, u32[]{:S(2)}) collective-permute-start(bf16[128,3584]{1,0:T(8,128)(2,1)} %tok_hbm.1), channel_id=1, source_target_pairs={{0,2},{2,0},{4,6},{6,4},{8,10},{10,8},{12,14},{14,12},{16,18},{18,... | collective-permute-start | bytes 2752520 | tf_op jit(solution)/shard_map/ppermute | solution.py:285
  0.5 2.8 %collective-permute-start = (s32[8,128]{1,0:T(8,128)}, s32[8,128]{1,0:T(8,128)S(1)}, u32[]{:S(2)}, u32[]{:S(2)}) collective-permute-start(s32[8,128]{1,0:T(8,128)} %bitcast.12), channel_id=1, source_target_pairs={{0,2},{2,0},{4,6},{6,4},{8,10},{10,8},{12,14},{14,12},{16,18},{18,... | collective-permute-start | bytes 12296 | tf_op jit(solution)/shard_map/ppermute | solution.py:285
  0.5 2.7 %collective-permute-start.1 = (f32[8,128]{1,0:T(8,128)}, f32[8,128]{1,0:T(8,128)S(1)}, u32[]{:S(2)}, u32[]{:S(2)}) collective-permute-start(f32[8,128]{1,0:T(8,128)} %bitcast.14), channel_id=1, source_target_pairs={{0,2},{2,0},{4,6},{6,4},{8,10},{10,8},{12,14},{14,12},{16,18},{18,... | collective-permute-start | bytes 12296 | tf_op jit(solution)/shard_map/ppermute | solution.py:285
  4.3 9.4 %collective-permute-start.3 = (bf16[16,3712]{1,0:T(8,128)(2,1)S(1)}, bf16[16,3712]{1,0:T(8,128)(2,1)S(1)}, u32[]{:S(2)}, u32[]{:S(2)}) collective-permute-start(bf16[16,3712]{1,0:T(8,128)(2,1)S(1)} %get-tuple-element.21), channel_id=1, source_target_pairs={{0,4},{2,6},{4,0},{6,2},{8,12},{10,14},{12,8},{14,10},{16,20},{18,... | collective-permute-start | bytes 356360 | tf_op jit(solution)/shard_map/ppermute | solution.py:285
  6.9 6.9 %collective-permute-start.4 = (bf16[16,3712]{1,0:T(8,128)(2,1)S(1)}, bf16[16,3712]{1,0:T(8,128)(2,1)S(1)}, u32[]{:S(2)}, u32[]{:S(2)}) collective-permute-start(bf16[16,3712]{1,0:T(8,128)(2,1)S(1)} %get-tuple-element.22), channel_id=1, source_target_pairs={{0,8},{2,10},{4,12},{6,14},{8,0},{10,2},{12,4},{14,6},{16,24},{18,... | collective-permute-start | bytes 356360 | tf_op jit(solution)/shard_map/ppermute | solution.py:285
  8.5 12.6 %collective-permute-start.9 = (bf16[16,3712]{1,0:T(8,128)(2,1)S(1)}, bf16[16,3712]{1,0:T(8,128)(2,1)S(1)}, u32[]{:S(2)}, u32[]{:S(2)}) collective-permute-start(bf16[16,3712]{1,0:T(8,128)(2,1)S(1)} %get-tuple-element.25), channel_id=1, source_target_pairs={{0,28},{2,30},{4,24},{6,26},{8,20},{10,22},{12,16},{14,18},{16,12}... | collective-permute-start | bytes 356360 | tf_op jit(solution)/shard_map/ppermute | solution.py:285
  10.9 13.8 %collective-permute-start.6 = (bf16[16,3712]{1,0:T(8,128)(2,1)S(1)}, bf16[16,3712]{1,0:T(8,128)(2,1)S(1)}, u32[]{:S(2)}, u32[]{:S(2)}) collective-permute-start(bf16[16,3712]{1,0:T(8,128)(2,1)S(1)} %get-tuple-element.23), channel_id=1, source_target_pairs={{0,12},{2,14},{4,8},{6,10},{8,4},{10,6},{12,0},{14,2},{16,28},{18,... | collective-permute-start | bytes 356360 | tf_op jit(solution)/shard_map/ppermute | solution.py:285
  12.5 13.7 %collective-permute-start.8 = (bf16[16,3712]{1,0:T(8,128)(2,1)S(1)}, bf16[16,3712]{1,0:T(8,128)(2,1)S(1)}, u32[]{:S(2)}, u32[]{:S(2)}) collective-permute-start(bf16[16,3712]{1,0:T(8,128)(2,1)S(1)} %get-tuple-element.24), channel_id=1, source_target_pairs={{0,16},{2,18},{4,20},{6,22},{8,24},{10,26},{12,28},{14,30},{16,0},... | collective-permute-start | bytes 356360 | tf_op jit(solution)/shard_map/ppermute | solution.py:285
  13.8 24.5 %collective-permute-start.5 = (bf16[48,3712]{1,0:T(8,128)(2,1)S(1)}, bf16[48,3712]{1,0:T(8,128)(2,1)S(1)}, u32[]{:S(2)}, u32[]{:S(2)}) collective-permute-start(bf16[48,3712]{1,0:T(8,128)(2,1)S(1)} %join.2), channel_id=1, source_target_pairs={{0,1},{1,0},{2,3},{3,2},{4,5},{5,4},{6,7},{7,6},{8,9},{9,8},{10,11... | collective-permute-start | bytes 1069064 | tf_op jit(solution)/shard_map/ppermute | solution.py:288
  15.4 14.6 %collective-permute-start.11 = (bf16[16,3712]{1,0:T(8,128)(2,1)S(1)}, bf16[16,3712]{1,0:T(8,128)(2,1)S(1)}, u32[]{:S(2)}, u32[]{:S(2)}) collective-permute-start(bf16[16,3712]{1,0:T(8,128)(2,1)S(1)} %get-tuple-element.27), channel_id=1, source_target_pairs={{0,20},{2,22},{4,16},{6,18},{8,28},{10,30},{12,24},{14,26},{16,4},... | collective-permute-start | bytes 356360 | tf_op jit(solution)/shard_map/ppermute | solution.py:285
  17.0 0.7 %copy-start = (s32[1,2,112,8]{2,3,1,0:T(8,128)S(1)}, s32[1,2,112,8]{2,3,1,0:T(8,128)}, u32[]{:S(2)}) copy-start(s32[1,2,112,8]{2,3,1,0:T(8,128)} %param.9) | copy-start | bytes 21508
  21.0 10.4 %collective-permute-start.13 = (bf16[16,3712]{1,0:T(8,128)(2,1)S(1)}, bf16[16,3712]{1,0:T(8,128)(2,1)S(1)}, u32[]{:S(2)}, u32[]{:S(2)}) collective-permute-start(bf16[16,3712]{1,0:T(8,128)(2,1)S(1)} %get-tuple-element.29), channel_id=1, source_target_pairs={{0,24},{2,26},{4,28},{6,30},{8,16},{10,18},{12,20},{14,22},{16,8},... | collective-permute-start | bytes 356360 | tf_op jit(solution)/shard_map/ppermute | solution.py:285
  24.7 6.7 %collective-permute-start.7 = (bf16[16,3712]{1,0:T(8,128)(2,1)S(1)}, bf16[16,3712]{1,0:T(8,128)(2,1)S(1)}, u32[]{:S(2)}, u32[]{:S(2)}) collective-permute-start(bf16[16,3712]{1,0:T(8,128)(2,1)S(1)} %collective-permute-done.6.refs_3_), channel_id=1, source_target_pairs={{0,1},{1,0},{2,3},{3,2},{4,5},{5,4},{6,7},{7,6},{8,9},{9,8},{10,11... | collective-permute-start | bytes 356360 | tf_op jit(solution)/shard_map/ppermute | solution.py:288
  26.2 10.8 %collective-permute-start.10 = (bf16[32,3712]{1,0:T(8,128)(2,1)S(1)}, bf16[32,3712]{1,0:T(8,128)(2,1)S(1)}, u32[]{:S(2)}, u32[]{:S(2)}) collective-permute-start(bf16[32,3712]{1,0:T(8,128)(2,1)S(1)} %join.3), channel_id=1, source_target_pairs={{0,1},{1,0},{2,3},{3,2},{4,5},{5,4},{6,7},{7,6},{8,9},{9,8},{10,11... | collective-permute-start | bytes 712712 | tf_op jit(solution)/shard_map/ppermute | solution.py:288
  29.9 7.0 %collective-permute-start.12 = (bf16[16,3712]{1,0:T(8,128)(2,1)S(1)}, bf16[16,3712]{1,0:T(8,128)(2,1)S(1)}, u32[]{:S(2)}, u32[]{:S(2)}) collective-permute-start(bf16[16,3712]{1,0:T(8,128)(2,1)S(1)} %collective-permute-done.11.refs_5_), channel_id=1, source_target_pairs={{0,1},{1,0},{2,3},{3,2},{4,5},{5,4},{6,7},{7,6},{8,9},{9,8},{10,11... | collective-permute-start | bytes 356360 | tf_op jit(solution)/shard_map/ppermute | solution.py:288
  31.4 6.8 %collective-permute-start.14 = (bf16[16,3712]{1,0:T(8,128)(2,1)S(1)}, bf16[16,3712]{1,0:T(8,128)(2,1)S(1)}, u32[]{:S(2)}, u32[]{:S(2)}) collective-permute-start(bf16[16,3712]{1,0:T(8,128)(2,1)S(1)} %collective-permute-done.13.refs_6_), channel_id=1, source_target_pairs={{0,1},{1,0},{2,3},{3,2},{4,5},{5,4},{6,7},{7,6},{8,9},{9,8},{10,11... | collective-permute-start | bytes 356360 | tf_op jit(solution)/shard_map/ppermute | solution.py:288

commit v3 on v2

--- a/solution.py
+++ b/solution.py
@@ -155,9 +155,11 @@
     )(place, *partner, own)
 
 
-def mask_kernel(m, keep_ref, mat_hbm, out_ref, mask_ref, sems):
-    parts = sems.shape[0]
+def mask_kernel(m, keep_hbm, mat_hbm, out_ref, keep_ref, mask_ref, sems):
+    parts = sems.shape[0] - 1
     units, depth = out_ref.shape[1], out_ref.shape[0] // parts
+    fetch_keep = pltpu.make_async_copy(keep_hbm.at[m], keep_ref, sems.at[parts])
+    fetch_keep.start()
     copies = [
         pltpu.make_async_copy(
             mat_hbm.at[m, pl.ds(p * depth, depth)], out_ref.at[pl.ds(p * depth, depth)], sems.at[p]
@@ -166,11 +168,12 @@
     ]
     for copy in copies:
         copy.start()
-    cols = keep_ref.shape[1]
+    cols = keep_ref.shape[0]
     lane = lax.broadcasted_iota(jnp.int32, (cols, units), 1) // BLOCK
     row = lax.broadcasted_iota(jnp.int32, (cols, units), 0)
+    fetch_keep.wait()
     mask_ref[...] = lax.dot_general(
-        keep_ref[m].astype(jnp.float32).astype(jnp.bfloat16),
+        keep_ref[...].astype(jnp.float32).astype(jnp.bfloat16),
         (lane == row).astype(jnp.bfloat16),
         (((0,), (0,)), ((), ())),
         preferred_element_type=jnp.float32,
@@ -186,38 +189,48 @@
             out_ref[span, :] = out_ref[span, :] * keep
 
 
-def mask_matrix(keep, matrices, m):
+def mask_matrix(keep, matrices, m, cost=0):
     rows, units = matrices.shape[1:]
     parts = next(p for p in (14, 16, 8, 7, 4, 2, 1) if rows % (p * BLOCK) == 0)
-    vmem = pl.BlockSpec(memory_space=pltpu.VMEM)
+    hbm = pl.BlockSpec(memory_space=pl.ANY)
     return pl.pallas_call(
         functools.partial(mask_kernel, m),
         out_shape=jax.ShapeDtypeStruct(matrices.shape[1:], matrices.dtype),
-        in_specs=[vmem, pl.BlockSpec(memory_space=pl.ANY)],
-        out_specs=vmem,
-        scratch_shapes=[pltpu.VMEM((rows // BLOCK, units), jnp.float32), pltpu.SemaphoreType.DMA((parts,))],
+        in_specs=[hbm, hbm],
+        out_specs=pl.BlockSpec(memory_space=pltpu.VMEM),
+        scratch_shapes=[
+            pltpu.VMEM(keep.shape[1:], keep.dtype),
+            pltpu.VMEM((rows // BLOCK, units), jnp.float32),
+            pltpu.SemaphoreType.DMA((parts + 1,)),
+        ],
         compiler_params=pltpu.CompilerParams(vmem_limit_bytes=10 << 20),
-        cost_estimate=pl.CostEstimate(flops=8 * rows * units, bytes_accessed=8 * rows * units, transcendentals=0),
+        cost_estimate=pl.CostEstimate(flops=0, bytes_accessed=cost, transcendentals=0),
         name="mask_matrix",
-    )(keep, pltpu.with_memory_space_constraint(matrices, pltpu.HBM))
-
-
-def join_kernel(*refs):
+    )(*(pltpu.with_memory_space_constraint(a, pltpu.HBM) for a in (keep, matrices)))
+
+
+def join_kernel(starts, *refs):
     *piece_refs, out_ref = refs
-    for k, piece_ref in enumerate(piece_refs):
-        out_ref[PAIR * k : PAIR * (k + 1)] = piece_ref[...]
-
-
-def join(*pieces):
+    width = out_ref.shape[1]
+    for k, (start, piece_ref) in enumerate(zip(starts, piece_refs)):
+        have = min(width, piece_ref.shape[1])
+        out_ref[PAIR * k : PAIR * (k + 1), :have] = piece_ref[start : start + PAIR, :have]
+        if have < width:
+            out_ref[PAIR * k : PAIR * (k + 1), have:] = jnp.zeros((PAIR, width - have), out_ref.dtype)
+
+
+def join(width, *pieces, cost=0):
+    pieces = [p if isinstance(p, tuple) else (p, 0) for p in pieces]
     vmem = pl.BlockSpec(memory_space=pltpu.VMEM)
     return pl.pallas_call(
-        join_kernel,
-        out_shape=jax.ShapeDtypeStruct((PAIR * len(pieces), pieces[0].shape[1]), pieces[0].dtype),
+        functools.partial(join_kernel, [start for _, start in pieces]),
+        out_shape=jax.ShapeDtypeStruct((PAIR * len(pieces), width), pieces[0][0].dtype),
         in_specs=[vmem] * len(pieces),
         out_specs=vmem,
         compiler_params=pltpu.CompilerParams(vmem_limit_bytes=4 << 20),
+        cost_estimate=pl.CostEstimate(flops=0, bytes_accessed=cost, transcendentals=0),
         name="join",
-    )(*pieces)
+    )(*(array for array, _ in pieces))
 
 
 def project_kernel(where, last, place, gate_ref, up_ref, *refs):
@@ -276,7 +289,6 @@
 def paired_form(tokens, route_ids, route_weight, gate_up, block_keep):
     n = lax.axis_size("expert")
     groups = n // 2
-    near = groups // 2
     me = lax.axis_index("expert")
     place = jnp.stack([me, lax.axis_index("tensor")]).astype(jnp.int32)
     width = tokens.shape[1]
@@ -294,25 +306,25 @@
     partner = [move(a, 1) for a in (ids, wgt, tokens)]
     piece = list(dispatch(place, ids, wgt, tokens, partner, groups))
     keep = jnp.swapaxes(block_keep[0], 1, 2)
-    got, other = [piece[0]] + [None] * (groups - 1), [None] * groups
+    got = [piece[0]] + [None] * (groups - 1)
+    got[1] = move(piece[1], 2)
+    block0 = cross(join(width, got[0], piece[2], cost=10 << 20))
+    got[3] = move(piece[3], 6)
+    got[7] = move(piece[7], 14)
     got[4] = move(piece[4], 8)
-    got[6] = move(piece[6], 12)
-    got[3] = move(piece[3], 6)
-    got[2] = move(piece[2], 4)
-    got[1] = move(piece[1], 2)
-    up = mask_matrix(after(keep, piece[0]), gate_up[0], 1)
-    got[7] = move(piece[7], 14)
-    got[5] = move(piece[5], 10)
-    gate = mask_matrix(after(keep, piece[0]), gate_up[0], 0)
-    block1 = cross(got[3])
-    block2 = cross(join(got[4], after(got[7], up)))
-    block0 = cross(join(got[0], got[1], got[2]))
-    block4 = cross(after(got[6], block1))
-    block3 = cross(after(got[5], up, got[7]))
+    got[2] = move(join(width + LANES, piece[2], (block0, 16), cost=10 << 20), 4)
+    gate = mask_matrix(after(keep, piece[0], got[1]), gate_up[0], 0, cost=30 << 20)
+    got[6] = move(after(piece[6], got[3]), 12)
+    block4 = cross(join(width, got[6], cost=10 << 20))
+    block1 = cross(join(width, got[1], got[3]))
+    got[5] = move(after(piece[5], got[4]), 10)
+    block2 = cross(join(width, got[4], got[7], cost=10 << 20))
+    up = mask_matrix(after(keep, piece[0], got[4]), gate_up[0], 1, cost=30 << 20)
+    block3 = cross(join(width, after(got[5], up), cost=10 << 20))
     masked = (gate, up)
     total, scale = project(place, masked, got, [(k, 0) for k in range(groups)], width)
-    where = [(0, 0), (0, 16), (0, 32), (1, 0), (2, 0), (3, 0), (4, 0), (2, 16)]
-    return project(place, masked, [block0, block1, block2, block3, block4], where, width, total, scale)
+    where = [(0, 0), (1, 0), (5, 16), (1, 16), (2, 0), (3, 0), (4, 0), (2, 16)]
+    return project(place, masked, [block0, block1, block2, block3, block4, got[2]], where, width, total, scale)
 
 
 def solution(mesh):

time: 40.8 us -> 39.6 us (0.971)
  starting transfers between devices: 22.7 us -> 19.1 us
  waiting for transfers between devices: 3.05 us -> 6.01 us
  local copies, waits for them, and re-layouts: 0.7 us -> 0 us
    ppermute x10, waiting for transfers between devices: 1.82 us -> 5.06 us  [move(): return lax.ppermute(a, 'expert', [(s, s ^ shift) for s in range(n)])]
    ppermute x10, starting transfers between devices: 15.7 us -> 13.2 us  [move(): return lax.ppermute(a, 'expert', [(s, s ^ shift) for s in range(n)])]
    ppermute x5, starting transfers between devices: 7.06 us -> 5.97 us  [cross(): return lax.ppermute(a, 'tensor', [(0, 1), (1, 0)])]
    unnamed x2 -> x0, local copies, waits for them, and re-layouts: 0.7 us -> none
  transfers between devices with their start and end apart: 15 -> 15, of which waited for: 3 -> 5; matrix products, arithmetic and copies ran while one was open for 0% -> 0% of each run, Pallas kernels for 26% -> 27%
where the time goes in v3:
time: 39.6 us; the launch traced here: 39.4 us
  starting transfers between devices  19.1 us (48%)
  Pallas kernels  14 us (35%)
  waiting for transfers between devices  6.01 us (15%)
    ppermute x10, starting transfers between devices, move(): return lax.ppermute(a, 'expert', [(s, s ^ shift) for s in range(n)])  13.2 us
    pallas_call x2, Pallas kernels, mask_matrix(): pl.pallas_call(functools.partial(mask_kernel, m), out_shape=jax.ShapeDtyp...  6.62 us
    ppermute x5, starting transfers between devices, cross(): return lax.ppermute(a, 'tensor', [(0, 1), (1, 0)])  5.97 us
    ppermute x10, waiting for transfers between devices, move(): return lax.ppermute(a, 'expert', [(s, s ^ shift) for s in range(n)])  5.06 us
    pallas_call x2, Pallas kernels, project(): pl.pallas_call(functools.partial(project_kernel, where, last), out_shape=...  4.08 us
    pallas_call x1, Pallas kernels, dispatch(): pl.pallas_call(functools.partial(own_kernel, groups), out_shape=jax.Shape...  2.17 us
    pallas_call x1, Pallas kernels, dispatch(): pl.pallas_call(functools.partial(pair_kernel, groups), out_shape=shapes,...  1.08 us
    ppermute x5, waiting for transfers between devices, cross(): return lax.ppermute(a, 'tensor', [(0, 1), (1, 0)])  0.95 us
  transfers between devices with their start and end apart: 15, of which 5 were waited for; matrix products, arithmetic and copies ran while one was open for 0% of the time, Pallas kernels for 27%

profile of v3, /device:TPU:0, one launch (start us, length us, event | category | flops | bytes accessed | tf_op | source)
XLA Modules:
  0.0 39.4 jit_solution(14448855860230330363)
XLA Ops:
  0.0 0.5 %collective-permute-start.2 = (bf16[128,3584]{1,0:T(8,128)(2,1)}, bf16[128,3584]{1,0:T(8,128)(2,1)S(1)}, u32[]{:S(2)}, u32[]{:S(2)}) collective-permute-start(bf16[128,3584]{1,0:T(8,128)(2,1)} %tok_hbm.1), channel_id=1, source_target_pairs={{0,2},{2,0},{4,6},{6,4},{8,10},{10,8},{12,14},{14,12},{16,18},{18,... | collective-permute-start | bytes 2752520 | tf_op jit(solution)/shard_map/ppermute | solution.py:297
  0.5 0.1 collective-permute-start
  0.5 0.5 %collective-permute-start.1 = (f32[8,128]{1,0:T(8,128)}, f32[8,128]{1,0:T(8,128)S(1)}, u32[]{:S(2)}, u32[]{:S(2)}) collective-permute-start(f32[8,128]{1,0:T(8,128)} %bitcast.14), channel_id=1, source_target_pairs={{0,2},{2,0},{4,6},{6,4},{8,10},{10,8},{12,14},{14,12},{16,18},{18,... | collective-permute-start | bytes 12296 | tf_op jit(solution)/shard_map/ppermute | solution.py:297
  1.0 0.1 pad_add_fusion.place
  1.0 2.2 %own_rows.1.own_ref = bf16[128,3712]{1,0:T(8,128)(2,1)S(1)} custom-call(s32[2]{0:T(128)S(1)} %pad_add_fusion.place, s32[8,128]{1,0:T(8,128)} %bitcast.13, f32[8,128]{1,0:T(8,128)} %bitcast.15, bf16[128,3584]{1,0:T(8,128)(2,1)} %tok_hbm.1), custom_call_target="tpu_custom_call" | custom-call | flops 117440512 | bytes 917504 | tf_op jit(solution)/shard_map/own_rows/pallas_call | solution.py:136
  3.2 0.0 collective-permute-done.ids_ref
  3.2 0.0 collective-permute-done.1.wgt_ref
  3.2 0.0 collective-permute-done.2.tok_ref
  3.3 1.1 %pair_rows.1 = (bf16[16,3712]{1,0:T(8,128)(2,1)S(1)}, bf16[16,3712]{1,0:T(8,128)(2,1)S(1)}, bf16[16,3712]{1,0:T(8,128)(2,1)S(1)}, bf16[16,3712]{1,0:T(8,128)(2,1...) custom-call(s32[2]{0:T(128)S(1)} %pad_add_fusion.place, ...), custom_call_target="tpu_custom_call" | custom-call | flops 117440512 | bytes 917504 | tf_op jit(solution)/shard_map/pair_rows/pallas_call | solution.py:147
  4.4 2.6 %collective-permute-start.5 = (bf16[32,3584]{1,0:T(8,128)(2,1)S(1)}, bf16[32,3584]{1,0:T(8,128)(2,1)S(1)}, u32[]{:S(2)}, u32[]{:S(2)}) collective-permute-start(bf16[32,3584]{1,0:T(8,128)(2,1)S(1)} %join.6), channel_id=1, source_target_pairs={{0,1},{1,0},{2,3},{3,2},{4,5},{5,4},{6,7},{7,6},{8,9},{9,8},{10,11... | collective-permute-start | bytes 688136 | tf_op jit(solution)/shard_map/ppermute | solution.py:300
  6.9 2.6 %collective-permute-start.4 = (bf16[16,3712]{1,0:T(8,128)(2,1)S(1)}, bf16[16,3712]{1,0:T(8,128)(2,1)S(1)}, u32[]{:S(2)}, u32[]{:S(2)}) collective-permute-start(bf16[16,3712]{1,0:T(8,128)(2,1)S(1)} %get-tuple-element.23), channel_id=1, source_target_pairs={{0,16},{2,18},{4,20},{6,22},{8,24},{10,26},{12,28},{14,30},{16,0},... | collective-permute-start | bytes 356360 | tf_op jit(solution)/shard_map/ppermute | solution.py:297
  9.5 2.5 %collective-permute-start.6 = (bf16[16,3712]{1,0:T(8,128)(2,1)S(1)}, bf16[16,3712]{1,0:T(8,128)(2,1)S(1)}, u32[]{:S(2)}, u32[]{:S(2)}) collective-permute-start(bf16[16,3712]{1,0:T(8,128)(2,1)S(1)} %get-tuple-element.26), channel_id=1, source_target_pairs={{0,12},{2,14},{4,8},{6,10},{8,4},{10,6},{12,0},{14,2},{16,28},{18,... | collective-permute-start | bytes 356360 | tf_op jit(solution)/shard_map/ppermute | solution.py:297
  12.0 0.5 %collective-permute-start.3 = (bf16[16,3712]{1,0:T(8,128)(2,1)S(1)}, bf16[16,3712]{1,0:T(8,128)(2,1)S(1)}, u32[]{:S(2)}, u32[]{:S(2)}) collective-permute-start(bf16[16,3712]{1,0:T(8,128)(2,1)S(1)} %get-tuple-element.21), channel_id=1, source_target_pairs={{0,4},{2,6},{4,0},{6,2},{8,12},{10,14},{12,8},{14,10},{16,20},{18,... | collective-permute-start | bytes 356360 | tf_op jit(solution)/shard_map/ppermute | solution.py:297
  12.6 1.2 %collective-permute-start.8 = (bf16[16,3712]{1,0:T(8,128)(2,1)S(1)}, bf16[16,3712]{1,0:T(8,128)(2,1)S(1)}, u32[]{:S(2)}, u32[]{:S(2)}) collective-permute-start(bf16[16,3712]{1,0:T(8,128)(2,1)S(1)} %get-tuple-element.27), channel_id=1, source_target_pairs={{0,28},{2,30},{4,24},{6,26},{8,20},{10,22},{12,16},{14,18},{16,12}... | collective-permute-start | bytes 356360 | tf_op jit(solution)/shard_map/ppermute | solution.py:297
  13.7 0.0 collective-permute-done.5.refs_1_.refs_0_
  13.7 1.4 %collective-permute-start.14 = (bf16[32,3712]{1,0:T(8,128)(2,1)S(1)}, bf16[32,3712]{1,0:T(8,128)(2,1)S(1)}, u32[]{:S(2)}, u32[]{:S(2)}) collective-permute-start(bf16[32,3712]{1,0:T(8,128)(2,1)S(1)} %join.11), channel_id=1, source_target_pairs={{0,8},{2,10},{4,12},{6,14},{8,0},{10,2},{12,4},{14,6},{16,24},{18,... | collective-permute-start | bytes 712712 | tf_op jit(solution)/shard_map/ppermute | solution.py:297
  15.1 1.0 %collective-permute-done.4.refs_0_.refs_4_ = bf16[16,3712]{1,0:T(8,128)(2,1)S(1)} collective-permute-done((bf16[16,3712]{1,0:T(8,128)(2,1)S(1)}, bf16[16,3712]{1,0:T(8,128)(2,1)S(1)}, u32[]{:S(2)}, u32[]{:S(2)}) %collective-permute-start.4) | collective-permute-done | bytes 118816 | tf_op jit(solution)/shard_map/ppermute | solution.py:297
  16.1 2.6 %collective-permute-start.10 = (bf16[16,3712]{1,0:T(8,128)(2,1)S(1)}, bf16[16,3712]{1,0:T(8,128)(2,1)S(1)}, u32[]{:S(2)}, u32[]{:S(2)}) collective-permute-start(bf16[16,3712]{1,0:T(8,128)(2,1)S(1)} %get-tuple-element.29), channel_id=1, source_target_pairs={{0,20},{2,22},{4,16},{6,18},{8,28},{10,30},{12,24},{14,26},{16,4},... | collective-permute-start | bytes 356360 | tf_op jit(solution)/shard_map/ppermute | solution.py:297
  18.6 0.0 collective-permute-done.6.refs_1_.refs_3_
  18.6 1.5 %collective-permute-start.12 = (bf16[16,3712]{1,0:T(8,128)(2,1)S(1)}, bf16[16,3712]{1,0:T(8,128)(2,1)S(1)}, u32[]{:S(2)}, u32[]{:S(2)}) collective-permute-start(bf16[16,3712]{1,0:T(8,128)(2,1)S(1)} %get-tuple-element.32), channel_id=1, source_target_pairs={{0,24},{2,26},{4,28},{6,30},{8,16},{10,18},{12,20},{14,22},{16,8},... | collective-permute-start | bytes 356360 | tf_op jit(solution)/shard_map/ppermute | solution.py:297
  20.1 0.0 collective-permute-done.3.refs_0_.refs_1_
  20.1 0.7 %collective-permute-start.7 = (bf16[32,3584]{1,0:T(8,128)(2,1)S(1)}, bf16[32,3584]{1,0:T(8,128)(2,1)S(1)}, u32[]{:S(2)}, u32[]{:S(2)}) collective-permute-start(bf16[32,3584]{1,0:T(8,128)(2,1)S(1)} %join.7), channel_id=1, source_target_pairs={{0,1},{1,0},{2,3},{3,2},{4,5},{5,4},{6,7},{7,6},{8,9},{9,8},{10,11... | collective-permute-start | bytes 688136 | tf_op jit(solution)/shard_map/ppermute | solution.py:300
  20.9 0.6 %collective-permute-done.8.refs_1_.refs_7_ = bf16[16,3712]{1,0:T(8,128)(2,1)S(1)} collective-permute-done((bf16[16,3712]{1,0:T(8,128)(2,1)S(1)}, bf16[16,3712]{1,0:T(8,128)(2,1)S(1)}, u32[]{:S(2)}, u32[]{:S(2)}) %collective-permute-start.8) | collective-permute-done | bytes 118816 | tf_op jit(solution)/shard_map/ppermute | solution.py:297
  21.5 0.8 %collective-permute-start.9 = (bf16[32,3584]{1,0:T(8,128)(2,1)S(1)}, bf16[32,3584]{1,0:T(8,128)(2,1)S(1)}, u32[]{:S(2)}, u32[]{:S(2)}) collective-permute-start(bf16[32,3584]{1,0:T(8,128)(2,1)S(1)} %join.8), channel_id=1, source_target_pairs={{0,1},{1,0},{2,3},{3,2},{4,5},{5,4},{6,7},{7,6},{8,9},{9,8},{10,11... | collective-permute-start | bytes 688136 | tf_op jit(solution)/shard_map/ppermute | solution.py:300
  22.3 3.3 %mask_matrix.3.up_ref = bf16[7168,512]{1,0:T(8,128)(2,1)S(1)} custom-call(s32[2,8,112]{2,1,0:T(8,128)} %bitcast.10, bf16[2,7168,512]{2,1,0:T(8,128)(2,1)} %bitcast.8), custom_call_target="tpu_custom_call" | custom-call | bytes 31457280 | tf_op jit(solution)/shard_map/mask_matrix/pallas_call | solution.py:196
  25.6 0.3 collective-permute-done.10.refs_0_.refs_5_
  26.0 1.0 %collective-permute-start.11 = (bf16[16,3584]{1,0:T(8,128)(2,1)S(1)}, bf16[16,3584]{1,0:T(8,128)(2,1)S(1)}, u32[]{:S(2)}, u32[]{:S(2)}) collective-permute-start(bf16[16,3584]{1,0:T(8,128)(2,1)S(1)} %join.9), channel_id=1, source_target_pairs={{0,1},{1,0},{2,3},{3,2},{4,5},{5,4},{6,7},{7,6},{8,9},{9,8},{10,11... | collective-permute-start | bytes 344072 | tf_op jit(solution)/shard_map/ppermute | solution.py:300
  27.0 3.1 %collective-permute-done.12.refs_0_.refs_6_ = bf16[16,3712]{1,0:T(8,128)(2,1)S(1)} collective-permute-done((bf16[16,3712]{1,0:T(8,128)(2,1)S(1)}, bf16[16,3712]{1,0:T(8,128)(2,1)S(1)}, u32[]{:S(2)}, u32[]{:S(2)}) %collective-permute-start.12) | collective-permute-done | bytes 118816 | tf_op jit(solution)/shard_map/ppermute | solution.py:297
  30.2 0.8 %collective-permute-start.13 = (bf16[16,3584]{1,0:T(8,128)(2,1)S(1)}, bf16[16,3584]{1,0:T(8,128)(2,1)S(1)}, u32[]{:S(2)}, u32[]{:S(2)}) collective-permute-start(bf16[16,3584]{1,0:T(8,128)(2,1)S(1)} %join.10), channel_id=1, source_target_pairs={{0,1},{1,0},{2,3},{3,2},{4,5},{5,4},{6,7},{7,6},{8,9},{9,8},{10,11... | collective-permute-start | bytes 344072 | tf_op jit(solution)/shard_map/ppermute | solution.py:300
  31.0 3.3 %mask_matrix.2.gate_ref = bf16[7168,512]{1,0:T(8,128)(2,1)S(1)} custom-call(s32[2,8,112]{2,1,0:T(8,128)} %bitcast.11, bf16[2,7168,512]{2,1,0:T(8,128)(2,1)} %bitcast.9), custom_call_target="tpu_custom_call" | custom-call | bytes 31457280 | tf_op jit(solution)/shard_map/mask_matrix/pallas_call | solution.py:196
  34.3 0.0 collective-permute-done.14.refs_2_.refs_5_
  34.3 1.7 %project_first.1 = (f32[2,128,512]{2,1,0:T(8,128)S(1)}, f32[128,128]{1,0:T(8,128)S(1)}) custom-call(s32[2]{0:T(128)S(1)} %pad_add_fusion.place, bf16[7168,512]{1,0:T(8,128)(2,1)S(1)} %mask_matrix.2.gate_ref, bf16[7168,512]{1,0:T(8,128)(2,1)S(1)} %mask_matrix.3.up_ref, bf16[16,3712]{1,0:T(8,128)(2,1)S(1)} %get-tuple-element.20.refs_0_, ...), custom_call_target="tpu_custom_call" | custom-call | flops 939524096 | bytes 7340032 | tf_op jit(solution)/shard_map/project_first/pallas_call | solution.py:275
  36.0 0.0 collective-permute-done.7.refs_1_
  36.1 0.0 collective-permute-done.9.refs_2_
  36.1 0.0 collective-permute-done.11.refs_3_
  36.1 0.9 %collective-permute-done.13.refs_4_ = bf16[16,3584]{1,0:T(8,128)(2,1)S(1)} collective-permute-done((bf16[16,3584]{1,0:T(8,128)(2,1)S(1)}, bf16[16,3584]{1,0:T(8,128)(2,1)S(1)}, u32[]{:S(2)}, u32[]{:S(2)}) %collective-permute-start.13) | collective-permute-done | bytes 114720 | tf_op jit(solution)/shard_map/ppermute | solution.py:300
  37.0 2.4 %project_last.1 = bf16[1,128,512]{2,1,0:T(8,128)(2,1)} custom-call(s32[2]{0:T(128)S(1)} %pad_add_fusion.place, bf16[7168,512]{1,0:T(8,128)(2,1)S(1)} %mask_matrix.2.gate_ref, bf16[7168,512]{1,0:T(8,128)(2,1)S(1)} %mask_matrix.3.up_ref, bf16[32,3584]{1,0:T(8,128)(2,1)S(1)} %collective-permute-done.5.refs_1_.refs_0_, ...), custom_call_target="tpu_custom_call" | custom-call | flops 939524096 | bytes 7340032 | tf_op jit(solution)/shard_map/project_last/pallas_call | solution.py:275
  (6 shorter events, 0.1 us)
Async XLA Ops:
  0.0 3.2 %collective-permute-start.2 = (bf16[128,3584]{1,0:T(8,128)(2,1)}, bf16[128,3584]{1,0:T(8,128)(2,1)S(1)}, u32[]{:S(2)}, u32[]{:S(2)}) collective-permute-start(bf16[128,3584]{1,0:T(8,128)(2,1)} %tok_hbm.1), channel_id=1, source_target_pairs={{0,2},{2,0},{4,6},{6,4},{8,10},{10,8},{12,14},{14,12},{16,18},{18,... | collective-permute-start | bytes 2752520 | tf_op jit(solution)/shard_map/ppermute | solution.py:297
  0.5 2.8 %collective-permute-start = (s32[8,128]{1,0:T(8,128)}, s32[8,128]{1,0:T(8,128)S(1)}, u32[]{:S(2)}, u32[]{:S(2)}) collective-permute-start(s32[8,128]{1,0:T(8,128)} %bitcast.12), channel_id=1, source_target_pairs={{0,2},{2,0},{4,6},{6,4},{8,10},{10,8},{12,14},{14,12},{16,18},{18,... | collective-permute-start | bytes 12296 | tf_op jit(solution)/shard_map/ppermute | solution.py:297
  0.5 2.7 %collective-permute-start.1 = (f32[8,128]{1,0:T(8,128)}, f32[8,128]{1,0:T(8,128)S(1)}, u32[]{:S(2)}, u32[]{:S(2)}) collective-permute-start(f32[8,128]{1,0:T(8,128)} %bitcast.14), channel_id=1, source_target_pairs={{0,2},{2,0},{4,6},{6,4},{8,10},{10,8},{12,14},{14,12},{16,18},{18,... | collective-permute-start | bytes 12296 | tf_op jit(solution)/shard_map/ppermute | solution.py:297
  4.4 9.4 %collective-permute-start.5 = (bf16[32,3584]{1,0:T(8,128)(2,1)S(1)}, bf16[32,3584]{1,0:T(8,128)(2,1)S(1)}, u32[]{:S(2)}, u32[]{:S(2)}) collective-permute-start(bf16[32,3584]{1,0:T(8,128)(2,1)S(1)} %join.6), channel_id=1, source_target_pairs={{0,1},{1,0},{2,3},{3,2},{4,5},{5,4},{6,7},{7,6},{8,9},{9,8},{10,11... | collective-permute-start | bytes 688136 | tf_op jit(solution)/shard_map/ppermute | solution.py:300
  6.9 9.1 %collective-permute-start.4 = (bf16[16,3712]{1,0:T(8,128)(2,1)S(1)}, bf16[16,3712]{1,0:T(8,128)(2,1)S(1)}, u32[]{:S(2)}, u32[]{:S(2)}) collective-permute-start(bf16[16,3712]{1,0:T(8,128)(2,1)S(1)} %get-tuple-element.23), channel_id=1, source_target_pairs={{0,16},{2,18},{4,20},{6,22},{8,24},{10,26},{12,28},{14,30},{16,0},... | collective-permute-start | bytes 356360 | tf_op jit(solution)/shard_map/ppermute | solution.py:297
  9.5 9.1 %collective-permute-start.6 = (bf16[16,3712]{1,0:T(8,128)(2,1)S(1)}, bf16[16,3712]{1,0:T(8,128)(2,1)S(1)}, u32[]{:S(2)}, u32[]{:S(2)}) collective-permute-start(bf16[16,3712]{1,0:T(8,128)(2,1)S(1)} %get-tuple-element.26), channel_id=1, source_target_pairs={{0,12},{2,14},{4,8},{6,10},{8,4},{10,6},{12,0},{14,2},{16,28},{18,... | collective-permute-start | bytes 356360 | tf_op jit(solution)/shard_map/ppermute | solution.py:297
  12.0 8.1 %collective-permute-start.3 = (bf16[16,3712]{1,0:T(8,128)(2,1)S(1)}, bf16[16,3712]{1,0:T(8,128)(2,1)S(1)}, u32[]{:S(2)}, u32[]{:S(2)}) collective-permute-start(bf16[16,3712]{1,0:T(8,128)(2,1)S(1)} %get-tuple-element.21), channel_id=1, source_target_pairs={{0,4},{2,6},{4,0},{6,2},{8,12},{10,14},{12,8},{14,10},{16,20},{18,... | collective-permute-start | bytes 356360 | tf_op jit(solution)/shard_map/ppermute | solution.py:297
  12.6 8.9 %collective-permute-start.8 = (bf16[16,3712]{1,0:T(8,128)(2,1)S(1)}, bf16[16,3712]{1,0:T(8,128)(2,1)S(1)}, u32[]{:S(2)}, u32[]{:S(2)}) collective-permute-start(bf16[16,3712]{1,0:T(8,128)(2,1)S(1)} %get-tuple-element.27), channel_id=1, source_target_pairs={{0,28},{2,30},{4,24},{6,26},{8,20},{10,22},{12,16},{14,18},{16,12}... | collective-permute-start | bytes 356360 | tf_op jit(solution)/shard_map/ppermute | solution.py:297
  13.7 20.6 %collective-permute-start.14 = (bf16[32,3712]{1,0:T(8,128)(2,1)S(1)}, bf16[32,3712]{1,0:T(8,128)(2,1)S(1)}, u32[]{:S(2)}, u32[]{:S(2)}) collective-permute-start(bf16[32,3712]{1,0:T(8,128)(2,1)S(1)} %join.11), channel_id=1, source_target_pairs={{0,8},{2,10},{4,12},{6,14},{8,0},{10,2},{12,4},{14,6},{16,24},{18,... | collective-permute-start | bytes 712712 | tf_op jit(solution)/shard_map/ppermute | solution.py:297
  16.1 9.9 %collective-permute-start.10 = (bf16[16,3712]{1,0:T(8,128)(2,1)S(1)}, bf16[16,3712]{1,0:T(8,128)(2,1)S(1)}, u32[]{:S(2)}, u32[]{:S(2)}) collective-permute-start(bf16[16,3712]{1,0:T(8,128)(2,1)S(1)} %get-tuple-element.29), channel_id=1, source_target_pairs={{0,20},{2,22},{4,16},{6,18},{8,28},{10,30},{12,24},{14,26},{16,4},... | collective-permute-start | bytes 356360 | tf_op jit(solution)/shard_map/ppermute | solution.py:297
  18.6 11.5 %collective-permute-start.12 = (bf16[16,3712]{1,0:T(8,128)(2,1)S(1)}, bf16[16,3712]{1,0:T(8,128)(2,1)S(1)}, u32[]{:S(2)}, u32[]{:S(2)}) collective-permute-start(bf16[16,3712]{1,0:T(8,128)(2,1)S(1)} %get-tuple-element.32), channel_id=1, source_target_pairs={{0,24},{2,26},{4,28},{6,30},{8,16},{10,18},{12,20},{14,22},{16,8},... | collective-permute-start | bytes 356360 | tf_op jit(solution)/shard_map/ppermute | solution.py:297
  20.1 15.9 %collective-permute-start.7 = (bf16[32,3584]{1,0:T(8,128)(2,1)S(1)}, bf16[32,3584]{1,0:T(8,128)(2,1)S(1)}, u32[]{:S(2)}, u32[]{:S(2)}) collective-permute-start(bf16[32,3584]{1,0:T(8,128)(2,1)S(1)} %join.7), channel_id=1, source_target_pairs={{0,1},{1,0},{2,3},{3,2},{4,5},{5,4},{6,7},{7,6},{8,9},{9,8},{10,11... | collective-permute-start | bytes 688136 | tf_op jit(solution)/shard_map/ppermute | solution.py:300
  21.5 14.6 %collective-permute-start.9 = (bf16[32,3584]{1,0:T(8,128)(2,1)S(1)}, bf16[32,3584]{1,0:T(8,128)(2,1)S(1)}, u32[]{:S(2)}, u32[]{:S(2)}) collective-permute-start(bf16[32,3584]{1,0:T(8,128)(2,1)S(1)} %join.8), channel_id=1, source_target_pairs={{0,1},{1,0},{2,3},{3,2},{4,5},{5,4},{6,7},{7,6},{8,9},{9,8},{10,11... | collective-permute-start | bytes 688136 | tf_op jit(solution)/shard_map/ppermute | solution.py:300
  26.0 10.1 %collective-permute-start.11 = (bf16[16,3584]{1,0:T(8,128)(2,1)S(1)}, bf16[16,3584]{1,0:T(8,128)(2,1)S(1)}, u32[]{:S(2)}, u32[]{:S(2)}) collective-permute-start(bf16[16,3584]{1,0:T(8,128)(2,1)S(1)} %join.9), channel_id=1, source_target_pairs={{0,1},{1,0},{2,3},{3,2},{4,5},{5,4},{6,7},{7,6},{8,9},{9,8},{10,11... | collective-permute-start | bytes 344072 | tf_op jit(solution)/shard_map/ppermute | solution.py:300
  30.2 6.9 %collective-permute-start.13 = (bf16[16,3584]{1,0:T(8,128)(2,1)S(1)}, bf16[16,3584]{1,0:T(8,128)(2,1)S(1)}, u32[]{:S(2)}, u32[]{:S(2)}) collective-permute-start(bf16[16,3584]{1,0:T(8,128)(2,1)S(1)} %join.10), channel_id=1, source_target_pairs={{0,1},{1,0},{2,3},{3,2},{4,5},{5,4},{6,7},{7,6},{8,9},{9,8},{10,11... | collective-permute-start | bytes 344072 | tf_op jit(solution)/shard_map/ppermute | solution.py:300

commit v4 on v3

--- a/solution.py
+++ b/solution.py
@@ -94,17 +94,19 @@
 
 
 def own_kernel(groups, place, ids_hbm, wgt_hbm, tok_hbm, out_ref, ids_ref, wgt_ref, tok_ref, sems):
-    copies = [
-        pltpu.make_async_copy(a, b, sems.at[i])
-        for i, (a, b) in enumerate(((ids_hbm, ids_ref), (wgt_hbm, wgt_ref), (tok_hbm, tok_ref)))
-    ]
+    count = tok_ref.shape[0]
+    part = count // (sems.shape[0] - 2)
+    pairs = [(ids_hbm, ids_ref), (wgt_hbm, wgt_ref)]
+    pairs += [(tok_hbm.at[pl.ds(at, part)], tok_ref.at[pl.ds(at, part)]) for at in range(0, count, part)]
+    copies = [pltpu.make_async_copy(a, b, sems.at[i]) for i, (a, b) in enumerate(pairs)]
     for copy in copies:
         copy.start()
     copies[0].wait()
     copies[1].wait()
     picks, weights = chosen_rows(groups, place, 0, ids_ref[...], wgt_ref[...])
     width = tok_ref.shape[1]
-    copies[2].wait()
+    for copy in copies[2:]:
+        copy.wait()
     for span in spans(width):
         got = jnp.dot(picks, tok_ref[:, span], preferred_element_type=jnp.float32)
         out_ref[:, span] = got.astype(out_ref.dtype)
@@ -138,7 +140,7 @@
         out_shape=jax.ShapeDtypeStruct((PAIR * groups, width + LANES), tok.dtype),
         in_specs=[smem, hbm, hbm, hbm],
         out_specs=vmem,
-        scratch_shapes=[pltpu.VMEM(a.shape, a.dtype) for a in (ids, wgt, tok)] + [pltpu.SemaphoreType.DMA((3,))],
+        scratch_shapes=[pltpu.VMEM(a.shape, a.dtype) for a in (ids, wgt, tok)] + [pltpu.SemaphoreType.DMA((2 + (4 if count % 64 == 0 else 1),))],
         compiler_params=pltpu.CompilerParams(vmem_limit_bytes=16 << 20),
         cost_estimate=cost,
         name="own_rows",

time: 39.6 us -> 39.8 us (level)
  no operation moved by 1% of the time
where the time goes in v4:
time: 39.8 us; the launch traced here: 39.5 us
  starting transfers between devices  19.1 us (48%)
  Pallas kernels  14.2 us (36%)
  waiting for transfers between devices  6.01 us (15%)
    ppermute x10, starting transfers between devices, move(): return lax.ppermute(a, 'expert', [(s, s ^ shift) for s in range(n)])  13.2 us
    pallas_call x2, Pallas kernels, mask_matrix(): pl.pallas_call(functools.partial(mask_kernel, m), out_shape=jax.ShapeDtyp...  6.62 us
    ppermute x5, starting transfers between devices, cross(): return lax.ppermute(a, 'tensor', [(0, 1), (1, 0)])  5.97 us
    ppermute x10, waiting for transfers between devices, move(): return lax.ppermute(a, 'expert', [(s, s ^ shift) for s in range(n)])  5.06 us
    pallas_call x2, Pallas kernels, project(): pl.pallas_call(functools.partial(project_kernel, where, last), out_shape=...  4.08 us
    pallas_call x1, Pallas kernels, dispatch(): pl.pallas_call(functools.partial(own_kernel, groups), out_shape=jax.Shape...  2.29 us
    pallas_call x1, Pallas kernels, dispatch(): pl.pallas_call(functools.partial(pair_kernel, groups), out_shape=shapes,...  1.08 us
    ppermute x5, waiting for transfers between devices, cross(): return lax.ppermute(a, 'tensor', [(0, 1), (1, 0)])  0.95 us
  transfers between devices with their start and end apart: 15, of which 5 were waited for; matrix products, arithmetic and copies ran while one was open for 0% of the time, Pallas kernels for 27%

profile of v4, /device:TPU:0, one launch (start us, length us, event | category | flops | bytes accessed | tf_op | source)
XLA Modules:
  0.0 39.5 jit_solution(11345976439255927745)
XLA Ops:
  0.0 0.5 %collective-permute-start.2 = (bf16[128,3584]{1,0:T(8,128)(2,1)}, bf16[128,3584]{1,0:T(8,128)(2,1)S(1)}, u32[]{:S(2)}, u32[]{:S(2)}) collective-permute-start(bf16[128,3584]{1,0:T(8,128)(2,1)} %tok_hbm.1), channel_id=1, source_target_pairs={{0,2},{2,0},{4,6},{6,4},{8,10},{10,8},{12,14},{14,12},{16,18},{18,... | collective-permute-start | bytes 2752520 | tf_op jit(solution)/shard_map/ppermute | solution.py:299
  0.5 0.1 collective-permute-start
  0.5 0.5 %collective-permute-start.1 = (f32[8,128]{1,0:T(8,128)}, f32[8,128]{1,0:T(8,128)S(1)}, u32[]{:S(2)}, u32[]{:S(2)}) collective-permute-start(f32[8,128]{1,0:T(8,128)} %bitcast.14), channel_id=1, source_target_pairs={{0,2},{2,0},{4,6},{6,4},{8,10},{10,8},{12,14},{14,12},{16,18},{18,... | collective-permute-start | bytes 12296 | tf_op jit(solution)/shard_map/ppermute | solution.py:299
  1.0 0.1 pad_add_fusion.place
  1.0 2.3 %own_rows.1.own_ref = bf16[128,3712]{1,0:T(8,128)(2,1)S(1)} custom-call(s32[2]{0:T(128)S(1)} %pad_add_fusion.place, s32[8,128]{1,0:T(8,128)} %bitcast.13, f32[8,128]{1,0:T(8,128)} %bitcast.15, bf16[128,3584]{1,0:T(8,128)(2,1)} %tok_hbm.1), custom_call_target="tpu_custom_call" | custom-call | flops 117440512 | bytes 917504 | tf_op jit(solution)/shard_map/own_rows/pallas_call | solution.py:138
  3.3 0.0 collective-permute-done.ids_ref
  3.4 0.0 collective-permute-done.1.wgt_ref
  3.4 0.0 collective-permute-done.2.tok_ref
  3.4 1.1 %pair_rows.1 = (bf16[16,3712]{1,0:T(8,128)(2,1)S(1)}, bf16[16,3712]{1,0:T(8,128)(2,1)S(1)}, bf16[16,3712]{1,0:T(8,128)(2,1)S(1)}, bf16[16,3712]{1,0:T(8,128)(2,1...) custom-call(s32[2]{0:T(128)S(1)} %pad_add_fusion.place, ...), custom_call_target="tpu_custom_call" | custom-call | flops 117440512 | bytes 917504 | tf_op jit(solution)/shard_map/pair_rows/pallas_call | solution.py:149
  4.5 2.6 %collective-permute-start.5 = (bf16[32,3584]{1,0:T(8,128)(2,1)S(1)}, bf16[32,3584]{1,0:T(8,128)(2,1)S(1)}, u32[]{:S(2)}, u32[]{:S(2)}) collective-permute-start(bf16[32,3584]{1,0:T(8,128)(2,1)S(1)} %join.6), channel_id=1, source_target_pairs={{0,1},{1,0},{2,3},{3,2},{4,5},{5,4},{6,7},{7,6},{8,9},{9,8},{10,11... | collective-permute-start | bytes 688136 | tf_op jit(solution)/shard_map/ppermute | solution.py:302
  7.1 2.6 %collective-permute-start.4 = (bf16[16,3712]{1,0:T(8,128)(2,1)S(1)}, bf16[16,3712]{1,0:T(8,128)(2,1)S(1)}, u32[]{:S(2)}, u32[]{:S(2)}) collective-permute-start(bf16[16,3712]{1,0:T(8,128)(2,1)S(1)} %get-tuple-element.23), channel_id=1, source_target_pairs={{0,16},{2,18},{4,20},{6,22},{8,24},{10,26},{12,28},{14,30},{16,0},... | collective-permute-start | bytes 356360 | tf_op jit(solution)/shard_map/ppermute | solution.py:299
  9.6 2.5 %collective-permute-start.6 = (bf16[16,3712]{1,0:T(8,128)(2,1)S(1)}, bf16[16,3712]{1,0:T(8,128)(2,1)S(1)}, u32[]{:S(2)}, u32[]{:S(2)}) collective-permute-start(bf16[16,3712]{1,0:T(8,128)(2,1)S(1)} %get-tuple-element.26), channel_id=1, source_target_pairs={{0,12},{2,14},{4,8},{6,10},{8,4},{10,6},{12,0},{14,2},{16,28},{18,... | collective-permute-start | bytes 356360 | tf_op jit(solution)/shard_map/ppermute | solution.py:299
  12.1 0.5 %collective-permute-start.3 = (bf16[16,3712]{1,0:T(8,128)(2,1)S(1)}, bf16[16,3712]{1,0:T(8,128)(2,1)S(1)}, u32[]{:S(2)}, u32[]{:S(2)}) collective-permute-start(bf16[16,3712]{1,0:T(8,128)(2,1)S(1)} %get-tuple-element.21), channel_id=1, source_target_pairs={{0,4},{2,6},{4,0},{6,2},{8,12},{10,14},{12,8},{14,10},{16,20},{18,... | collective-permute-start | bytes 356360 | tf_op jit(solution)/shard_map/ppermute | solution.py:299
  12.7 1.2 %collective-permute-start.8 = (bf16[16,3712]{1,0:T(8,128)(2,1)S(1)}, bf16[16,3712]{1,0:T(8,128)(2,1)S(1)}, u32[]{:S(2)}, u32[]{:S(2)}) collective-permute-start(bf16[16,3712]{1,0:T(8,128)(2,1)S(1)} %get-tuple-element.27), channel_id=1, source_target_pairs={{0,28},{2,30},{4,24},{6,26},{8,20},{10,22},{12,16},{14,18},{16,12}... | collective-permute-start | bytes 356360 | tf_op jit(solution)/shard_map/ppermute | solution.py:299
  13.8 0.0 collective-permute-done.5.refs_1_.refs_0_
  13.9 1.4 %collective-permute-start.14 = (bf16[32,3712]{1,0:T(8,128)(2,1)S(1)}, bf16[32,3712]{1,0:T(8,128)(2,1)S(1)}, u32[]{:S(2)}, u32[]{:S(2)}) collective-permute-start(bf16[32,3712]{1,0:T(8,128)(2,1)S(1)} %join.11), channel_id=1, source_target_pairs={{0,8},{2,10},{4,12},{6,14},{8,0},{10,2},{12,4},{14,6},{16,24},{18,... | collective-permute-start | bytes 712712 | tf_op jit(solution)/shard_map/ppermute | solution.py:299
  15.2 1.0 %collective-permute-done.4.refs_0_.refs_4_ = bf16[16,3712]{1,0:T(8,128)(2,1)S(1)} collective-permute-done((bf16[16,3712]{1,0:T(8,128)(2,1)S(1)}, bf16[16,3712]{1,0:T(8,128)(2,1)S(1)}, u32[]{:S(2)}, u32[]{:S(2)}) %collective-permute-start.4) | collective-permute-done | bytes 118816 | tf_op jit(solution)/shard_map/ppermute | solution.py:299
  16.2 2.6 %collective-permute-start.10 = (bf16[16,3712]{1,0:T(8,128)(2,1)S(1)}, bf16[16,3712]{1,0:T(8,128)(2,1)S(1)}, u32[]{:S(2)}, u32[]{:S(2)}) collective-permute-start(bf16[16,3712]{1,0:T(8,128)(2,1)S(1)} %get-tuple-element.29), channel_id=1, source_target_pairs={{0,20},{2,22},{4,16},{6,18},{8,28},{10,30},{12,24},{14,26},{16,4},... | collective-permute-start | bytes 356360 | tf_op jit(solution)/shard_map/ppermute | solution.py:299
  18.7 0.0 collective-permute-done.6.refs_1_.refs_3_
  18.8 1.5 %collective-permute-start.12 = (bf16[16,3712]{1,0:T(8,128)(2,1)S(1)}, bf16[16,3712]{1,0:T(8,128)(2,1)S(1)}, u32[]{:S(2)}, u32[]{:S(2)}) collective-permute-start(bf16[16,3712]{1,0:T(8,128)(2,1)S(1)} %get-tuple-element.32), channel_id=1, source_target_pairs={{0,24},{2,26},{4,28},{6,30},{8,16},{10,18},{12,20},{14,22},{16,8},... | collective-permute-start | bytes 356360 | tf_op jit(solution)/shard_map/ppermute | solution.py:299
  20.2 0.0 collective-permute-done.3.refs_0_.refs_1_
  20.2 0.7 %collective-permute-start.7 = (bf16[32,3584]{1,0:T(8,128)(2,1)S(1)}, bf16[32,3584]{1,0:T(8,128)(2,1)S(1)}, u32[]{:S(2)}, u32[]{:S(2)}) collective-permute-start(bf16[32,3584]{1,0:T(8,128)(2,1)S(1)} %join.7), channel_id=1, source_target_pairs={{0,1},{1,0},{2,3},{3,2},{4,5},{5,4},{6,7},{7,6},{8,9},{9,8},{10,11... | collective-permute-start | bytes 688136 | tf_op jit(solution)/shard_map/ppermute | solution.py:302
  21.0 0.6 %collective-permute-done.8.refs_1_.refs_7_ = bf16[16,3712]{1,0:T(8,128)(2,1)S(1)} collective-permute-done((bf16[16,3712]{1,0:T(8,128)(2,1)S(1)}, bf16[16,3712]{1,0:T(8,128)(2,1)S(1)}, u32[]{:S(2)}, u32[]{:S(2)}) %collective-permute-start.8) | collective-permute-done | bytes 118816 | tf_op jit(solution)/shard_map/ppermute | solution.py:299
  21.6 0.8 %collective-permute-start.9 = (bf16[32,3584]{1,0:T(8,128)(2,1)S(1)}, bf16[32,3584]{1,0:T(8,128)(2,1)S(1)}, u32[]{:S(2)}, u32[]{:S(2)}) collective-permute-start(bf16[32,3584]{1,0:T(8,128)(2,1)S(1)} %join.8), channel_id=1, source_target_pairs={{0,1},{1,0},{2,3},{3,2},{4,5},{5,4},{6,7},{7,6},{8,9},{9,8},{10,11... | collective-permute-start | bytes 688136 | tf_op jit(solution)/shard_map/ppermute | solution.py:302
  22.4 3.3 %mask_matrix.3.up_ref = bf16[7168,512]{1,0:T(8,128)(2,1)S(1)} custom-call(s32[2,8,112]{2,1,0:T(8,128)} %bitcast.10, bf16[2,7168,512]{2,1,0:T(8,128)(2,1)} %bitcast.8), custom_call_target="tpu_custom_call" | custom-call | bytes 31457280 | tf_op jit(solution)/shard_map/mask_matrix/pallas_call | solution.py:198
  25.7 0.3 collective-permute-done.10.refs_0_.refs_5_
  26.1 1.0 %collective-permute-start.11 = (bf16[16,3584]{1,0:T(8,128)(2,1)S(1)}, bf16[16,3584]{1,0:T(8,128)(2,1)S(1)}, u32[]{:S(2)}, u32[]{:S(2)}) collective-permute-start(bf16[16,3584]{1,0:T(8,128)(2,1)S(1)} %join.9), channel_id=1, source_target_pairs={{0,1},{1,0},{2,3},{3,2},{4,5},{5,4},{6,7},{7,6},{8,9},{9,8},{10,11... | collective-permute-start | bytes 344072 | tf_op jit(solution)/shard_map/ppermute | solution.py:302
  27.1 3.1 %collective-permute-done.12.refs_0_.refs_6_ = bf16[16,3712]{1,0:T(8,128)(2,1)S(1)} collective-permute-done((bf16[16,3712]{1,0:T(8,128)(2,1)S(1)}, bf16[16,3712]{1,0:T(8,128)(2,1)S(1)}, u32[]{:S(2)}, u32[]{:S(2)}) %collective-permute-start.12) | collective-permute-done | bytes 118816 | tf_op jit(solution)/shard_map/ppermute | solution.py:299
  30.3 0.8 %collective-permute-start.13 = (bf16[16,3584]{1,0:T(8,128)(2,1)S(1)}, bf16[16,3584]{1,0:T(8,128)(2,1)S(1)}, u32[]{:S(2)}, u32[]{:S(2)}) collective-permute-start(bf16[16,3584]{1,0:T(8,128)(2,1)S(1)} %join.10), channel_id=1, source_target_pairs={{0,1},{1,0},{2,3},{3,2},{4,5},{5,4},{6,7},{7,6},{8,9},{9,8},{10,11... | collective-permute-start | bytes 344072 | tf_op jit(solution)/shard_map/ppermute | solution.py:302
  31.1 3.3 %mask_matrix.2.gate_ref = bf16[7168,512]{1,0:T(8,128)(2,1)S(1)} custom-call(s32[2,8,112]{2,1,0:T(8,128)} %bitcast.11, bf16[2,7168,512]{2,1,0:T(8,128)(2,1)} %bitcast.9), custom_call_target="tpu_custom_call" | custom-call | bytes 31457280 | tf_op jit(solution)/shard_map/mask_matrix/pallas_call | solution.py:198
  34.4 0.0 collective-permute-done.14.refs_2_.refs_5_
  34.4 1.7 %project_first.1 = (f32[2,128,512]{2,1,0:T(8,128)S(1)}, f32[128,128]{1,0:T(8,128)S(1)}) custom-call(s32[2]{0:T(128)S(1)} %pad_add_fusion.place, bf16[7168,512]{1,0:T(8,128)(2,1)S(1)} %mask_matrix.2.gate_ref, bf16[7168,512]{1,0:T(8,128)(2,1)S(1)} %mask_matrix.3.up_ref, bf16[16,3712]{1,0:T(8,128)(2,1)S(1)} %get-tuple-element.20.refs_0_, ...), custom_call_target="tpu_custom_call" | custom-call | flops 939524096 | bytes 7340032 | tf_op jit(solution)/shard_map/project_first/pallas_call | solution.py:277
  36.2 0.0 collective-permute-done.7.refs_1_
  36.2 0.0 collective-permute-done.9.refs_2_
  36.2 0.0 collective-permute-done.11.refs_3_
  36.2 0.9 %collective-permute-done.13.refs_4_ = bf16[16,3584]{1,0:T(8,128)(2,1)S(1)} collective-permute-done((bf16[16,3584]{1,0:T(8,128)(2,1)S(1)}, bf16[16,3584]{1,0:T(8,128)(2,1)S(1)}, u32[]{:S(2)}, u32[]{:S(2)}) %collective-permute-start.13) | collective-permute-done | bytes 114720 | tf_op jit(solution)/shard_map/ppermute | solution.py:302
  37.1 2.4 %project_last.1 = bf16[1,128,512]{2,1,0:T(8,128)(2,1)} custom-call(s32[2]{0:T(128)S(1)} %pad_add_fusion.place, bf16[7168,512]{1,0:T(8,128)(2,1)S(1)} %mask_matrix.2.gate_ref, bf16[7168,512]{1,0:T(8,128)(2,1)S(1)} %mask_matrix.3.up_ref, bf16[32,3584]{1,0:T(8,128)(2,1)S(1)} %collective-permute-done.5.refs_1_.refs_0_, ...), custom_call_target="tpu_custom_call" | custom-call | flops 939524096 | bytes 7340032 | tf_op jit(solution)/shard_map/project_last/pallas_call | solution.py:277
  (6 shorter events, 0.1 us)
Async XLA Ops:
  0.0 3.4 %collective-permute-start.2 = (bf16[128,3584]{1,0:T(8,128)(2,1)}, bf16[128,3584]{1,0:T(8,128)(2,1)S(1)}, u32[]{:S(2)}, u32[]{:S(2)}) collective-permute-start(bf16[128,3584]{1,0:T(8,128)(2,1)} %tok_hbm.1), channel_id=1, source_target_pairs={{0,2},{2,0},{4,6},{6,4},{8,10},{10,8},{12,14},{14,12},{16,18},{18,... | collective-permute-start | bytes 2752520 | tf_op jit(solution)/shard_map/ppermute | solution.py:299
  0.5 2.9 %collective-permute-start = (s32[8,128]{1,0:T(8,128)}, s32[8,128]{1,0:T(8,128)S(1)}, u32[]{:S(2)}, u32[]{:S(2)}) collective-permute-start(s32[8,128]{1,0:T(8,128)} %bitcast.12), channel_id=1, source_target_pairs={{0,2},{2,0},{4,6},{6,4},{8,10},{10,8},{12,14},{14,12},{16,18},{18,... | collective-permute-start | bytes 12296 | tf_op jit(solution)/shard_map/ppermute | solution.py:299
  0.5 2.8 %collective-permute-start.1 = (f32[8,128]{1,0:T(8,128)}, f32[8,128]{1,0:T(8,128)S(1)}, u32[]{:S(2)}, u32[]{:S(2)}) collective-permute-start(f32[8,128]{1,0:T(8,128)} %bitcast.14), channel_id=1, source_target_pairs={{0,2},{2,0},{4,6},{6,4},{8,10},{10,8},{12,14},{14,12},{16,18},{18,... | collective-permute-start | bytes 12296 | tf_op jit(solution)/shard_map/ppermute | solution.py:299
  4.5 9.4 %collective-permute-start.5 = (bf16[32,3584]{1,0:T(8,128)(2,1)S(1)}, bf16[32,3584]{1,0:T(8,128)(2,1)S(1)}, u32[]{:S(2)}, u32[]{:S(2)}) collective-permute-start(bf16[32,3584]{1,0:T(8,128)(2,1)S(1)} %join.6), channel_id=1, source_target_pairs={{0,1},{1,0},{2,3},{3,2},{4,5},{5,4},{6,7},{7,6},{8,9},{9,8},{10,11... | collective-permute-start | bytes 688136 | tf_op jit(solution)/shard_map/ppermute | solution.py:302
  7.1 9.1 %collective-permute-start.4 = (bf16[16,3712]{1,0:T(8,128)(2,1)S(1)}, bf16[16,3712]{1,0:T(8,128)(2,1)S(1)}, u32[]{:S(2)}, u32[]{:S(2)}) collective-permute-start(bf16[16,3712]{1,0:T(8,128)(2,1)S(1)} %get-tuple-element.23), channel_id=1, source_target_pairs={{0,16},{2,18},{4,20},{6,22},{8,24},{10,26},{12,28},{14,30},{16,0},... | collective-permute-start | bytes 356360 | tf_op jit(solution)/shard_map/ppermute | solution.py:299
  9.6 9.1 %collective-permute-start.6 = (bf16[16,3712]{1,0:T(8,128)(2,1)S(1)}, bf16[16,3712]{1,0:T(8,128)(2,1)S(1)}, u32[]{:S(2)}, u32[]{:S(2)}) collective-permute-start(bf16[16,3712]{1,0:T(8,128)(2,1)S(1)} %get-tuple-element.26), channel_id=1, source_target_pairs={{0,12},{2,14},{4,8},{6,10},{8,4},{10,6},{12,0},{14,2},{16,28},{18,... | collective-permute-start | bytes 356360 | tf_op jit(solution)/shard_map/ppermute | solution.py:299
  12.1 8.1 %collective-permute-start.3 = (bf16[16,3712]{1,0:T(8,128)(2,1)S(1)}, bf16[16,3712]{1,0:T(8,128)(2,1)S(1)}, u32[]{:S(2)}, u32[]{:S(2)}) collective-permute-start(bf16[16,3712]{1,0:T(8,128)(2,1)S(1)} %get-tuple-element.21), channel_id=1, source_target_pairs={{0,4},{2,6},{4,0},{6,2},{8,12},{10,14},{12,8},{14,10},{16,20},{18,... | collective-permute-start | bytes 356360 | tf_op jit(solution)/shard_map/ppermute | solution.py:299
  12.7 8.9 %collective-permute-start.8 = (bf16[16,3712]{1,0:T(8,128)(2,1)S(1)}, bf16[16,3712]{1,0:T(8,128)(2,1)S(1)}, u32[]{:S(2)}, u32[]{:S(2)}) collective-permute-start(bf16[16,3712]{1,0:T(8,128)(2,1)S(1)} %get-tuple-element.27), channel_id=1, source_target_pairs={{0,28},{2,30},{4,24},{6,26},{8,20},{10,22},{12,16},{14,18},{16,12}... | collective-permute-start | bytes 356360 | tf_op jit(solution)/shard_map/ppermute | solution.py:299
  13.9 20.6 %collective-permute-start.14 = (bf16[32,3712]{1,0:T(8,128)(2,1)S(1)}, bf16[32,3712]{1,0:T(8,128)(2,1)S(1)}, u32[]{:S(2)}, u32[]{:S(2)}) collective-permute-start(bf16[32,3712]{1,0:T(8,128)(2,1)S(1)} %join.11), channel_id=1, source_target_pairs={{0,8},{2,10},{4,12},{6,14},{8,0},{10,2},{12,4},{14,6},{16,24},{18,... | collective-permute-start | bytes 712712 | tf_op jit(solution)/shard_map/ppermute | solution.py:299
  16.2 9.9 %collective-permute-start.10 = (bf16[16,3712]{1,0:T(8,128)(2,1)S(1)}, bf16[16,3712]{1,0:T(8,128)(2,1)S(1)}, u32[]{:S(2)}, u32[]{:S(2)}) collective-permute-start(bf16[16,3712]{1,0:T(8,128)(2,1)S(1)} %get-tuple-element.29), channel_id=1, source_target_pairs={{0,20},{2,22},{4,16},{6,18},{8,28},{10,30},{12,24},{14,26},{16,4},... | collective-permute-start | bytes 356360 | tf_op jit(solution)/shard_map/ppermute | solution.py:299
  18.8 11.5 %collective-permute-start.12 = (bf16[16,3712]{1,0:T(8,128)(2,1)S(1)}, bf16[16,3712]{1,0:T(8,128)(2,1)S(1)}, u32[]{:S(2)}, u32[]{:S(2)}) collective-permute-start(bf16[16,3712]{1,0:T(8,128)(2,1)S(1)} %get-tuple-element.32), channel_id=1, source_target_pairs={{0,24},{2,26},{4,28},{6,30},{8,16},{10,18},{12,20},{14,22},{16,8},... | collective-permute-start | bytes 356360 | tf_op jit(solution)/shard_map/ppermute | solution.py:299
  20.2 15.9 %collective-permute-start.7 = (bf16[32,3584]{1,0:T(8,128)(2,1)S(1)}, bf16[32,3584]{1,0:T(8,128)(2,1)S(1)}, u32[]{:S(2)}, u32[]{:S(2)}) collective-permute-start(bf16[32,3584]{1,0:T(8,128)(2,1)S(1)} %join.7), channel_id=1, source_target_pairs={{0,1},{1,0},{2,3},{3,2},{4,5},{5,4},{6,7},{7,6},{8,9},{9,8},{10,11... | collective-permute-start | bytes 688136 | tf_op jit(solution)/shard_map/ppermute | solution.py:302
  21.6 14.6 %collective-permute-start.9 = (bf16[32,3584]{1,0:T(8,128)(2,1)S(1)}, bf16[32,3584]{1,0:T(8,128)(2,1)S(1)}, u32[]{:S(2)}, u32[]{:S(2)}) collective-permute-start(bf16[32,3584]{1,0:T(8,128)(2,1)S(1)} %join.8), channel_id=1, source_target_pairs={{0,1},{1,0},{2,3},{3,2},{4,5},{5,4},{6,7},{7,6},{8,9},{9,8},{10,11... | collective-permute-start | bytes 688136 | tf_op jit(solution)/shard_map/ppermute | solution.py:302
  26.1 10.1 %collective-permute-start.11 = (bf16[16,3584]{1,0:T(8,128)(2,1)S(1)}, bf16[16,3584]{1,0:T(8,128)(2,1)S(1)}, u32[]{:S(2)}, u32[]{:S(2)}) collective-permute-start(bf16[16,3584]{1,0:T(8,128)(2,1)S(1)} %join.9), channel_id=1, source_target_pairs={{0,1},{1,0},{2,3},{3,2},{4,5},{5,4},{6,7},{7,6},{8,9},{9,8},{10,11... | collective-permute-start | bytes 344072 | tf_op jit(solution)/shard_map/ppermute | solution.py:302
  30.3 6.9 %collective-permute-start.13 = (bf16[16,3584]{1,0:T(8,128)(2,1)S(1)}, bf16[16,3584]{1,0:T(8,128)(2,1)S(1)}, u32[]{:S(2)}, u32[]{:S(2)}) collective-permute-start(bf16[16,3584]{1,0:T(8,128)(2,1)S(1)} %join.10), channel_id=1, source_target_pairs={{0,1},{1,0},{2,3},{3,2},{4,5},{5,4},{6,7},{7,6},{8,9},{9,8},{10,11... | collective-permute-start | bytes 344072 | tf_op jit(solution)/shard_map/ppermute | solution.py:302
